TPU v7x, 32 devices: a whole 2x2x4 slice. The times are simulated.
32 devices in a mesh: dp: 16 (over z, y, core), blk: 2 (over x).
Axes of the slice: x: 2, y: 2, z: 4, core: 2. Of those that a mesh axis runs over, the one named last changes fastest.
Arguments:
- hidden: bfloat16 [64, 512, 768], P('dp', 'blk'), may hold values from -6 to 6
- lengths: int32 [64, 2], P('dp'), may hold values from 1 to 512, as said below
- flags: int32 [64], P('dp'), may hold values from 0 to 1
- buckets: int32 [1023], replicated, may hold values from 0 to 31
- g_attn: float32 [768], replicated, may hold values from 0.5 to 1.5
- w_query: bfloat16 [768, 768], replicated, may hold values from -0.21875 to 0.21875
- w_key: bfloat16 [768, 768], replicated, may hold values from -0.21875 to 0.21875
- w_value: bfloat16 [768, 768], replicated, may hold values from -0.21875 to 0.21875
- w_out: bfloat16 [768, 768], replicated, may hold values from -0.625 to 0.625
- g_ffn: float32 [768], replicated, may hold values from 0.5 to 1.5
- w_in: bfloat16 [768, 3072], replicated, may hold values from -0.21875 to 0.21875
- w_ffn_out: bfloat16 [3072, 768], replicated, may hold values from -0.109375 to 0.109375
- bias_table: float32 [32, 12], replicated, may hold values from -4 to 4
- cotangent: bfloat16 [64, 512, 768], P('dp', 'blk'), may hold values from -6 to 6
Outputs:
- output: bfloat16 [64, 512, 768], P('dp', 'blk')
- input_grad: bfloat16 [64, 512, 768], P('dp', 'blk')
- g_attn_grad: float32 [768], P('dp')
- query_grad: float32 [768, 768], P('dp')
- key_grad: float32 [768, 768], P('dp')
- value_grad: float32 [768, 768], P('dp')
- out_grad: float32 [768, 768], P('dp')
- g_ffn_grad: float32 [768], P('dp')
- in_grad: float32 [768, 3072], P('dp')
- ffn_out_grad: float32 [3072, 768], P('dp')
- table_grad: float32 [32, 12], replicated
Inputs may be any that keep to these rules, and one draw needn't show every extreme that they name: In each aligned group of 4 sequences, one, drawn from the seed, has both lengths equal to 512.
All inputs are finite; a program needn't handle non-finite values.
Results may differ from a plain program's by a relative error of at most 0.017.
Values may be sent and summed in bfloat16 or wider, within the bound.
No kernel may reach another device: no remote copies, remote signals or barrier semaphores. Data moves between devices by JAX's collectives and lax.ppermute only.
A program may use at most 256 MiB of HBM per device.

v0:
```python
import copy
import functools
import math

import jax
import jax.numpy as jnp
from jax import lax
from jax.experimental import pallas as pl
from jax.experimental.pallas import tpu as pltpu
from jax.sharding import PartitionSpec as P

EPSILON = 1e-06
MASKED = -1000000000.0
SCALING = 0.125
LOG2E = 1.4426950408889634
LN2 = 0.6931471805599453
HEAD = 64
LANES = 128
VMEM_LIMIT = 32 * 2**20
BF16 = jnp.bfloat16
F32 = jnp.float32


def dot(left, right, left_dim, right_dim):
    return lax.dot_general(
        left, right, (((left_dim,), (right_dim,)), ((), ())), preferred_element_type=F32
    )


RESIDENT = pl.BlockSpec(memory_space=pltpu.VMEM)


def in_hbm(values):
    return pltpu.with_memory_space_constraint(values, pltpu.HBM)


def resident(*values):
    return [pltpu.with_memory_space_constraint(v, pltpu.VMEM) for v in values]


def expand_kernel(vector_ref, out_ref):
    group, _, width = vector_ref.shape
    for head in range(group):
        rows = jnp.broadcast_to(vector_ref[head], (LANES, width))
        moved = pltpu.roll(rows, 0, 1, stride=1, stride_axis=0)
        out_ref[head] = moved[:, : out_ref.shape[2]]


def expand_bias(vector, width):
    heads, length = vector.shape
    group = 4 if heads % 4 == 0 else 1
    return pl.pallas_call(
        expand_kernel,
        grid=(heads // group,),
        in_specs=[pl.BlockSpec((group, 1, length), lambda h: (h, 0, 0))],
        out_specs=pl.BlockSpec((group, LANES, width), lambda h: (h, 0, 0)),
        out_shape=jax.ShapeDtypeStruct((heads, LANES, width), F32),
        compiler_params=pltpu.CompilerParams(vmem_limit_bytes=VMEM_LIMIT),
    )(vector.reshape(heads, 1, length))


def fold_kernel(grad_ref, out_ref):
    width = grad_ref.shape[2]
    length = out_ref.shape[2]
    pad = jnp.zeros((8, length - width), F32)
    for head in range(grad_ref.shape[0]):
        total = jnp.zeros((8, length), F32)
        for start in range(0, LANES, 8):
            rows = jnp.concatenate([grad_ref[head, start : start + 8, :], pad], axis=1)
            total = total + pltpu.roll(rows, LANES - 8 - start, 1)
        folded = total[7:8]
        for row in range(7):
            folded = folded + pltpu.roll(total[row : row + 1], 7 - row, 1)
        out_ref[head] = jnp.broadcast_to(folded, (8, length))


def fold_bias(grad, length):
    heads, _, width = grad.shape
    group = 4 if heads % 4 == 0 else 1
    return pl.pallas_call(
        fold_kernel,
        grid=(heads // group,),
        in_specs=[pl.BlockSpec((group, LANES, width), lambda h: (h, 0, 0))],
        out_specs=pl.BlockSpec((group, 8, length), lambda h: (h, 0, 0)),
        out_shape=jax.ShapeDtypeStruct((heads, 8, length), F32),
        compiler_params=pltpu.CompilerParams(vmem_limit_bytes=VMEM_LIMIT),
        cost_estimate=pl.CostEstimate(flops=0, bytes_accessed=0, transcendentals=0),
    )(in_hbm(grad))[:, 0]


def inverse_of(values):
    return lax.rsqrt(jnp.mean(values * values, axis=1, keepdims=True) + EPSILON)


def project_kernel(scalars, kept_ref, got_ref, gain_ref, w_ref, hidden_ref, attn_in_ref, out_ref):
    half = kept_ref.shape[1]
    step = pl.program_id(0)

    @pl.when(step == 0)
    def _():
        for ref, place in ((kept_ref, scalars[1]), (got_ref, 1 - scalars[1])):
            rows = pl.ds(pl.multiple_of(place * half, half), half)
            hidden_ref[rows, :] = ref[0]
            values = ref[0].astype(F32)
            attn_in_ref[rows, :] = (values * inverse_of(values) * gain_ref[...]).astype(BF16)

    scale = jnp.where(step == 0, SCALING * LOG2E, 1.0)
    out_ref[0] = (dot(attn_in_ref[...], w_ref[0], 1, 0) * scale).astype(BF16)


def project(scalars, kept, got, gain, weights):
    _, half, width = kept.shape
    count = 2 * half
    once = pl.Buffered(1)

    def whole(*shape):
        return pl.BlockSpec(shape, lambda j, *_: (0,) * len(shape), pipeline_mode=once)

    return pl.pallas_call(
        project_kernel,
        grid_spec=pltpu.PrefetchScalarGridSpec(
            num_scalar_prefetch=1,
            grid=(weights.shape[0],),
            in_specs=[
                whole(1, half, width),
                whole(1, half, width),
                whole(1, width),
                pl.BlockSpec((1, width, width), lambda j, *_: (j, 0, 0)),
            ],
            out_specs=[
                whole(count, width),
                whole(count, width),
                pl.BlockSpec((1, count, width), lambda j, *_: (j, 0, 0)),
            ],
        ),
        out_shape=[
            jax.ShapeDtypeStruct((count, width), BF16),
            jax.ShapeDtypeStruct((count, width), BF16),
            jax.ShapeDtypeStruct((weights.shape[0], count, width), BF16),
        ],
        compiler_params=pltpu.CompilerParams(vmem_limit_bytes=VMEM_LIMIT),
        cost_estimate=pl.CostEstimate(
            flops=6 * count * width * width, bytes_accessed=8 * 2**20, transcendentals=0
        ),
    )(scalars, kept, got, gain.reshape(1, width), weights)


def attend_kernel(
    valid, q_ref, k_ref, v_ref, bias_ref, out_ref, copy_ref, weights_ref, inverse_ref, *, chunk, seq
):
    limit = valid[seq]
    count = q_ref.shape[1]
    pair = pl.program_id(0)
    columns = pl.ds(pl.multiple_of(pair * LANES, LANES), LANES)
    queries, keys, values = (ref[0].astype(F32) for ref in (q_ref, k_ref, v_ref))
    lane = lax.broadcasted_iota(jnp.int32, (count, LANES), 1)
    row = lax.broadcasted_iota(jnp.int32, (count, LANES), 0)
    heads = []
    for head in range(2):
        mine = (lane // HEAD) == head
        extra = lane == (1 - head) * HEAD
        mask = jnp.where(extra & (row >= limit), MASKED, 0.0)
        heads.append(
            (
                jnp.where(mine, queries, jnp.where(extra, 1.0, 0.0)).astype(BF16),
                jnp.where(mine, keys, mask).astype(BF16),
                jnp.where(mine, values, 1.0).astype(BF16),
            )
        )
    first = lax.broadcasted_iota(jnp.int32, (chunk, LANES), 1) < HEAD
    units = [(step, head) for step in range(count // chunk) for head in range(2)]

    def scores(unit):
        step, head = unit
        rows = slice(step * chunk, (step + 1) * chunk)
        windows = [
            bias_ref[head, :, count - LANES * (1 + block) : 2 * count - LANES * (1 + block)]
            for block in range(step * chunk // LANES, (step + 1) * chunk // LANES)
        ]
        return dot(heads[head][0][rows], heads[head][1], 1, 1) + jnp.concatenate(windows, axis=0)

    ahead = 2
    logits = {unit: scores(unit) for unit in units[:ahead]}
    sums = {}
    for place, unit in enumerate(units):
        step, head = unit
        rows = slice(step * chunk, (step + 1) * chunk)
        if place + ahead < len(units):
            logits[units[place + ahead]] = scores(units[place + ahead])
        top = jnp.max(logits[unit], axis=1, keepdims=True)
        weights = jnp.exp2(logits[unit] - top).astype(BF16)
        weights_ref[head, rows, :] = weights
        sums[unit] = dot(weights, heads[head][2], 1, 0)
        if head == 1:
            one, two = sums[step, 0], sums[step, 1]
            inverse = 1.0 / pltpu.roll(jnp.where(first, two, one), HEAD, 1)
            inverse_ref[rows, :] = inverse
            context = (jnp.where(first, one, two) * inverse).astype(BF16)
            out_ref[rows, columns] = context
            copy_ref[rows, :] = context


def projections_of(count, pair):
    return [
        pl.BlockSpec((1, count, LANES), lambda *at, part=part: (part, 0, pair(*at)))
        for part in range(3)
    ]


def attend(projected, bias, valid, seq, chunk=256):
    _, count, width = projected.shape
    block = pl.BlockSpec((count, LANES), lambda p, *_: (0, p))
    return pl.pallas_call(
        functools.partial(attend_kernel, chunk=chunk, seq=seq),
        grid_spec=pltpu.PrefetchScalarGridSpec(
            num_scalar_prefetch=1,
            grid=(width // LANES,),
            in_specs=[
                *projections_of(count, lambda p, *_: p),
                pl.BlockSpec((2, LANES, bias.shape[2]), lambda p, *_: (p, 0, 0)),
            ],
            out_specs=[
                RESIDENT,
                block,
                pl.BlockSpec((2, count, count), lambda p, *_: (p, 0, 0)),
                block,
            ],
        ),
        out_shape=[
            pltpu.VMEM((count, width), BF16),
            pltpu.HBM((count, width), BF16),
            pltpu.HBM((width // HEAD, count, count), BF16),
            pltpu.HBM((count, width), F32),
        ],
        compiler_params=pltpu.CompilerParams(vmem_limit_bytes=VMEM_LIMIT),
        cost_estimate=pl.CostEstimate(
            flops=32 * count * count * width, bytes_accessed=12 * 2**20, transcendentals=0
        ),
    )(valid, *[projected] * 3, bias)


def store_shares(grad, core, sent_ref, kept_ref, start=0, folds=1):
    count, rows, width = sent_ref.shape
    grad = grad.astype(BF16) if rows % 16 == 0 else grad
    for group in range(count):
        for fold in range(folds):
            place = (2 * group * folds + fold) * rows
            even = grad[place : place + rows]
            place += folds * rows
            odd = grad[place : place + rows]
            at = fold * (width // folds) + start
            columns = slice(at, at + grad.shape[1])
            sent_ref[group, :, columns] = jnp.where(core == 0, odd, even).astype(BF16)
            kept_ref[group, :, columns] = jnp.where(core == 0, even, odd).astype(BF16)


def attend_back_kernel(scalars, *refs, seqs, steps, finish):
    refs = list(refs)

    def some(count):
        taken = refs[:count]
        del refs[:count]
        return taken

    projected_refs = [some(3) for _ in range(seqs)]
    weights_refs, inverse_refs = some(seqs), some(seqs)
    attn_in_refs = some(seqs)
    ctx_refs = some(seqs)
    grad_ref, wq_ref, wk_ref, wv_ref = some(4)
    if finish:
        before_ref, hidden_ref, mid_ref, gain_ref = some(4)
    bias_ref, sent_ref, kept_ref = some(3)
    if finish:
        in_kept_ref, in_sent_ref, grad_gain_ref, back_ref = some(4)
    else:
        out_ref, back_ref = some(2)
    core, own = scalars[0], scalars[1]
    count = projected_refs[0][0].shape[1]
    lane = lax.broadcasted_iota(jnp.int32, (count, LANES), 1)

    step = pl.program_id(0)

    @pl.when(step == 0)
    def _():
        back_ref[...] = jnp.zeros_like(back_ref)

    @pl.when(step < steps)
    def _():
        bias_ref[...] = jnp.zeros_like(bias_ref)
        projections = jnp.concatenate([wq_ref[...], wk_ref[...], wv_ref[...]], axis=1)
        units = [(seq, head) for seq in range(seqs) for head in range(2)]
        loaded, scored, low_grads, parts = {}, {}, {}, {}

        def load(seq):
            here = slice(seq * count, (seq + 1) * count)
            queries, keys, values = (ref[0].astype(F32) for ref in projected_refs[seq])
            grads = grad_ref[here, :].astype(F32) * inverse_refs[seq][...]
            products = grads * ctx_refs[seq][...].astype(F32)
            turned = jnp.transpose(queries).astype(BF16), jnp.transpose(grads).astype(BF16)
            loaded[seq] = keys, values, grads, products, turned

        def score(unit):
            seq, head = unit
            if head == 0:
                load(seq)
            _, values, grads, products, _ = loaded[seq]
            mine = (lane // HEAD) == head
            other = (1 - head) * HEAD
            extra = (lane == other) | (lane == other + 1)
            v_head = jnp.where(mine, values, jnp.where(extra, 1.0, 0.0)).astype(BF16)
            delta = jnp.sum(jnp.where(mine, products, 0.0), axis=1, keepdims=True)
            high = delta.astype(BF16).astype(F32)
            spread = jnp.where(lane == other, -high, jnp.where(extra, high - delta, 0.0))
            g_head = jnp.where(mine, grads, spread).astype(BF16)
            scored[unit] = dot(g_head, v_head, 1, 1)

        def weigh(unit):
            seq, head = unit
            grad_logits = weights_refs[seq][head].astype(F32) * scored[unit]
            blocks = count // LANES
            for tile in range(2 * blocks - 1):
                bias_ref[head, :, tile * LANES : (tile + 1) * LANES] += sum(
                    grad_logits[
                        block * LANES : (block + 1) * LANES,
                        (tile + 1 + block - blocks) * LANES : (tile + 2 + block - blocks) * LANES,
                    ]
                    for block in range(blocks)
                    if 0 <= tile + 1 + block - blocks < blocks
                )
            low_grads[unit] = grad_logits.astype(BF16)

        def multiply(unit):
            seq, head = unit
            keys, _, _, _, (queries_t, grads_t) = loaded[seq]
            rows = slice(head * HEAD, (head + 1) * HEAD)
            k_head = jnp.where((lane // HEAD) == head, keys, 0.0).astype(BF16)
            low = low_grads[unit]
            parts[unit] = (
                dot(low, k_head, 1, 0),
                dot(queries_t[rows], low, 1, 0),
                dot(grads_t[rows], weights_refs[seq][head], 1, 0),
            )

        def project(seq):
            here = slice(seq * count, (seq + 1) * count)
            one, two = parts[seq, 0], parts[seq, 1]
            dk = jnp.transpose(jnp.concatenate([one[1], two[1]], axis=0))
            dv = jnp.transpose(jnp.concatenate([one[2], two[2]], axis=0))
            all_grads = jnp.concatenate(
                [(SCALING * (one[0] + two[0])).astype(BF16), (LN2 * dk).astype(BF16), dv.astype(BF16)],
                axis=1,
            )
            back_ref[here, :] += dot(all_grads, projections, 1, 1)
            return dot(attn_in_refs[seq][...], all_grads, 0, 0)

        weight_grad = None
        for place in range(len(units) + 1):
            if place < len(units):
                score(units[place])
            if 0 <= place - 1 < len(units):
                weigh(units[place - 1])
            if 0 <= place - 1:
                seq, head = units[place - 1]
                multiply((seq, head))
                if head == 1:
                    part = project(seq)
                    weight_grad = part if weight_grad is None else weight_grad + part
        store_shares(weight_grad, core, sent_ref, kept_ref)

    @pl.when(step >= steps)
    def _():
        place = step - steps
        half = count // 2
        if not finish:
            out_ref[...] = back_ref[pl.ds(pl.multiple_of(place * half, half), half), :].astype(BF16)
        else:
            start = pl.multiple_of(row_block(place, own, seqs) * half, half)
            back = back_ref[pl.ds(start, half), :] + before_ref[...].astype(F32)
            values = hidden_ref[...].astype(F32)
            inverse = lax.rsqrt(jnp.mean(values * values, axis=1, keepdims=True) + EPSILON)
            normed = values * inverse
            grad_gain = jnp.sum(back * normed, axis=0, keepdims=True)
            back = back * gain_ref[...]
            mean = jnp.mean(back * normed, axis=1, keepdims=True)
            grad = mid_ref[...].astype(F32) + inverse * (back - normed * mean)

            @pl.when(place == 0)
            def _():
                grad_gain_ref[...] = grad_gain

            @pl.when(place > 0)
            def _():
                grad_gain_ref[...] += grad_gain

            @pl.when(place < seqs)
            def _():
                in_sent_ref[0] = grad.astype(BF16)

            @pl.when(place >= seqs)
            def _():
                in_kept_ref[0] = grad.astype(BF16)


def row_block(place, own, seqs):
    return 2 * lax.rem(place, seqs) + jnp.where(place < seqs, 1 - own, own)


def attend_back(
    scalars, saved, attn_in, grads, projections, bias_width, pairs, ends
):
    seqs = len(saved)
    _, count, width = saved[0][0].shape
    size = lax.axis_size("dp")
    rows = width // size
    half = count // 2
    first, last = pairs
    steps = last - first
    once = pl.Buffered(1)

    def early(p):
        return jnp.minimum(p, steps - 1)

    def late(p):
        return jnp.maximum(p - steps, 0)

    weight = pl.BlockSpec((width, LANES), lambda p, *_: (0, first + early(p)))
    probs = pl.BlockSpec((2, count, count), lambda p, *_: (first + early(p), 0, 0))
    shares = pl.BlockSpec((size // 2, rows, 3 * LANES), lambda p, *_: (0, 0, early(p)))
    row = pl.BlockSpec((1, width), lambda p, *_: (0, 0), pipeline_mode=once)

    block = pl.BlockSpec((count, LANES), lambda p, *_: (0, first + early(p)))
    tall = pl.BlockSpec((seqs * count, LANES), lambda p, *_: (0, first + early(p)))
    whole = pl.BlockSpec((count, width), lambda p, *_: (0, 0), pipeline_mode=once)
    projected, contexts, weights, inverses = zip(*saved)
    operands = [v for v in projected for _ in range(3)]
    operands += [*weights, *inverses, *attn_in, *contexts, grads]
    operands = [in_hbm(v) for v in (*operands, *projections)]
    specs = projections_of(count, lambda p, *_: first + early(p)) * seqs
    specs += [probs] * seqs + [block] * seqs + [whole] * seqs
    specs += [block] * seqs + [tall] + [weight] * 3
    share = pltpu.HBM((size // 2, rows, 3 * LANES * steps), BF16)
    out_shape = [pltpu.HBM((2 * steps, LANES, bias_width), F32), share, share]
    out_specs = [pl.BlockSpec((2, LANES, bias_width), lambda p, *_: (early(p), 0, 0)), shares, shares]
    if ends is not None:
        before, hidden, grad_mid, gain = ends
        operands += [in_hbm(before), in_hbm(hidden), in_hbm(grad_mid), gain.reshape(1, width)]
        mixed_up = pl.BlockSpec(
            (half, width), lambda p, scalars: (row_block(late(p), scalars[1], seqs), 0)
        )
        specs += [mixed_up] * 3 + [row]
        out_shape.append(pltpu.HBM((2 * seqs, half, width), BF16))
        out_shape.append(pltpu.HBM((seqs, half, width), BF16))
        out_shape.append(jax.ShapeDtypeStruct((1, width), F32))
        out_specs += [
            pl.BlockSpec(
                (1, half, width),
                lambda p, scalars: (scalars[1] * seqs + jnp.maximum(late(p) - seqs, 0), 0, 0),
            ),
            pl.BlockSpec((1, half, width), lambda p, *_: (jnp.minimum(late(p), seqs - 1), 0, 0)),
            row,
        ]
    else:
        out_shape.append(pltpu.HBM((seqs * count, width), BF16))
        out_specs.append(pl.BlockSpec((half, width), lambda p, *_: (late(p), 0)))
    return pl.pallas_call(
        functools.partial(attend_back_kernel, seqs=seqs, steps=steps, finish=ends is not None),
        grid_spec=pltpu.PrefetchScalarGridSpec(
            num_scalar_prefetch=1,
            grid=(steps + 2 * seqs,),
            in_specs=specs,
            out_specs=out_specs,
            scratch_shapes=[pltpu.VMEM((seqs * count, width), F32)],
        ),
        out_shape=out_shape,
        compiler_params=pltpu.CompilerParams(vmem_limit_bytes=VMEM_LIMIT),
        cost_estimate=pl.CostEstimate(flops=0, bytes_accessed=0, transcendentals=0),
    )(scalars, *operands)


def store_product(left, right, core, sent_ref, kept_ref, folds=1, columns=256):
    for start in range(0, right.shape[1], columns):
        grad = dot(left, right[:, start : start + columns], 0, 0)
        store_shares(grad, core, sent_ref, kept_ref, start, folds)


def in_weight_kernel(scalars, ffn_in_ref, pre_ref, sent_ref, kept_ref):
    width = sent_ref.shape[2]
    columns = pl.ds(pl.multiple_of(pl.program_id(0) * width, width), width)
    store_product(ffn_in_ref[...], pre_ref[:, columns], scalars[0], sent_ref, kept_ref)


def in_weights(scalars, ffn_in, grad_pre):
    tokens, width = ffn_in.shape
    steps = grad_pre.shape[1] // width
    size = lax.axis_size("dp")
    share = pl.BlockSpec((size // 2, width // size, width), lambda j, *_: (0, 0, j))
    return pl.pallas_call(
        in_weight_kernel,
        grid_spec=pltpu.PrefetchScalarGridSpec(
            num_scalar_prefetch=1,
            grid=(steps,),
            in_specs=[RESIDENT, RESIDENT],
            out_specs=[share, share],
        ),
        out_shape=[pltpu.HBM((size // 2, width // size, steps * width), BF16)] * 2,
        compiler_params=pltpu.CompilerParams(vmem_limit_bytes=VMEM_LIMIT),
        cost_estimate=pl.CostEstimate(flops=0, bytes_accessed=0, transcendentals=0),
    )(scalars, *resident(ffn_in, grad_pre))


def out_weight_kernel(scalars, act_ref, upstream_ref, sent_ref, kept_ref, *, folds):
    width = upstream_ref.shape[1]
    columns = pl.ds(pl.multiple_of(pl.program_id(0) * width, width), width)
    store_product(act_ref[:, columns], upstream_ref[...], scalars[0], sent_ref, kept_ref, folds)


def out_weights(scalars, act, upstream):
    tokens, width = upstream.shape
    units = act.shape[1]
    size = lax.axis_size("dp")
    folds = steps = units // width
    shape = (size // 2, width // size, units)
    share = pl.BlockSpec((size // 2 // steps,) + shape[1:], lambda j, *_: (j, 0, 0))
    return pl.pallas_call(
        functools.partial(out_weight_kernel, folds=folds),
        grid_spec=pltpu.PrefetchScalarGridSpec(
            num_scalar_prefetch=1,
            grid=(steps,),
            in_specs=[RESIDENT, RESIDENT],
            out_specs=[share, share],
        ),
        out_shape=[pltpu.HBM(shape, BF16)] * 2,
        compiler_params=pltpu.CompilerParams(vmem_limit_bytes=VMEM_LIMIT),
        cost_estimate=pl.CostEstimate(flops=0, bytes_accessed=0, transcendentals=0),
    )(scalars, *resident(act, upstream))


def middle_kernel(scalars, *refs, seqs, chunk):
    context_refs, hidden_refs = refs[:seqs], refs[seqs : 2 * seqs]
    upstream_ref, w_out_ref, gain_ref, w_in_ref, w_ffn_out_ref = refs[2 * seqs : 2 * seqs + 5]
    act_ref, grad_pre_ref, ffn_in_ref, out_kept_ref, out_sent_ref = refs[2 * seqs + 5 : 2 * seqs + 10]
    grad_low_ref, grad_context_ref, sent_ref, kept_ref, grad_gain_ref = refs[
        2 * seqs + 10 : 2 * seqs + 15
    ]
    mixed_ref, total_ref, back_ref = refs[2 * seqs + 15 :]
    tokens, width = mixed_ref.shape
    count = tokens // seqs
    columns = w_in_ref.shape[1]
    step = pl.program_id(0)
    here = pl.ds(pl.multiple_of(step * columns, columns), columns)
    pieces = [
        (slice(start, start + chunk), start // count, slice(start % count, start % count + chunk))
        for start in range(0, tokens, chunk)
    ]

    @pl.when(step == 0)
    def _():
        for rows, seq, local in pieces:
            mixed = hidden_refs[seq][local, :].astype(F32)
            mixed = mixed + dot(context_refs[seq][local, :], w_out_ref[...], 1, 0)
            mixed_ref[rows, :] = mixed
            total_ref[rows, :] = mixed
            back_ref[rows, :] = jnp.zeros((chunk, width), F32)
            ffn_in_ref[rows, :] = (mixed * inverse_of(mixed) * gain_ref[...]).astype(BF16)

    for rows, _, _ in pieces:
        pre = dot(ffn_in_ref[rows, :], w_in_ref[...], 1, 0)
        grad_act = dot(upstream_ref[rows, :], w_ffn_out_ref[...], 1, 1)
        below = 0.5 + 0.5 * lax.erf(pre * 0.7071067811865476)
        density = jnp.exp2(pre * pre * (-0.5 * LOG2E)) * 0.3989422804014327
        act = (pre * below).astype(BF16)
        grad_pre = (grad_act * (below + pre * density)).astype(BF16)
        act_ref[rows, here] = act
        grad_pre_ref[rows, here] = grad_pre
        total_ref[rows, :] += dot(act, w_ffn_out_ref[...], 1, 0)
        back_ref[rows, :] += dot(grad_pre, w_in_ref[...], 1, 1)

    @pl.when(step == pl.num_programs(0) - 1)
    def _():
        grad_gain = jnp.zeros(gain_ref.shape, F32)
        weight = None
        for rows, seq, local in pieces:
            half, local_half = local.start // (count // 2), slice(
                local.start % (count // 2), local.start % (count // 2) + chunk
            )
            layer_out = total_ref[rows, :].astype(BF16)

            @pl.when(scalars[1] == half)
            def _():
                out_kept_ref[scalars[1] * seqs + seq, local_half, :] = layer_out

            @pl.when(scalars[1] != half)
            def _():
                out_sent_ref[seq, local_half, :] = layer_out

            mixed = mixed_ref[rows, :]
            inverse = inverse_of(mixed)
            normed = mixed * inverse
            back = back_ref[rows, :]
            grad_gain += jnp.sum(back * normed, axis=0, keepdims=True)
            back = back * gain_ref[...]
            mean = jnp.mean(back * normed, axis=1, keepdims=True)
            grad = upstream_ref[rows, :].astype(F32) + inverse * (back - normed * mean)
            low = grad.astype(BF16)
            grad_low_ref[rows, :] = low
            grad_context_ref[rows, :] = dot(low, w_out_ref[...], 1, 1).astype(BF16)
            part = dot(context_refs[seq][local, :], low, 0, 0)
            weight = part if weight is None else weight + part
        grad_gain_ref[...] = grad_gain
        store_shares(weight, scalars[0], sent_ref, kept_ref)


def middle(
    scalars, contexts, hidden, upstream, w_out, gain, w_in, w_ffn_out, columns=512, chunk=256
):
    tokens, width = upstream.shape
    units = w_in.shape[1]
    seqs = len(contexts)
    size = lax.axis_size("dp")
    once = pl.Buffered(1)

    def whole(*shape):
        return pl.BlockSpec(shape, lambda j, *_: (0,) * len(shape), pipeline_mode=once)

    shares = (size // 2, width // size, width)
    low = pltpu.HBM((tokens, width), BF16)
    return pl.pallas_call(
        functools.partial(middle_kernel, seqs=seqs, chunk=chunk),
        grid_spec=pltpu.PrefetchScalarGridSpec(
            num_scalar_prefetch=1,
            grid=(units // columns,),
            in_specs=[RESIDENT] * (2 * seqs + 1)
            + [
                whole(width, width),
                whole(1, width),
                pl.BlockSpec((width, columns), lambda j, *_: (0, j)),
                pl.BlockSpec((columns, width), lambda j, *_: (j, 0)),
            ],
            out_specs=[RESIDENT] * 3
            + [whole(2 * seqs, tokens // seqs // 2, width), whole(seqs, tokens // seqs // 2, width)]
            + [whole(tokens, width)] * 2
            + [whole(*shares), whole(*shares), whole(1, width)],
            scratch_shapes=[pltpu.VMEM((tokens, width), F32)] * 3,
        ),
        out_shape=[
            pltpu.VMEM((tokens, units), BF16),
            pltpu.VMEM((tokens, units), BF16),
            pltpu.VMEM((tokens, width), BF16),
            pltpu.HBM((2 * seqs, tokens // seqs // 2, width), BF16),
            pltpu.HBM((seqs, tokens // seqs // 2, width), BF16),
            low,
            low,
        ]
        + [pltpu.HBM(shares, BF16)] * 2
        + [jax.ShapeDtypeStruct((1, width), F32)],
        compiler_params=pltpu.CompilerParams(vmem_limit_bytes=VMEM_LIMIT),
        cost_estimate=pl.CostEstimate(
            flops=8 * tokens * width * units, bytes_accessed=20 * 2**20, transcendentals=0
        ),
    )(
        scalars,
        *resident(*contexts, *hidden, upstream),
        in_hbm(w_out),
        gain.reshape(1, width),
        in_hbm(w_in),
        in_hbm(w_ffn_out),
    )


def bits_of(size):
    return size.bit_length() - 1


def flip(axis, mask):
    size = lax.axis_size(axis)
    return [(index, index ^ mask) for index in range(size)]


def swap_blk(values):
    return lax.ppermute(values, "blk", flip("blk", 1))


def pick(values, index, axis):
    return lax.dynamic_index_in_dim(values, index, axis, keepdims=False)


def part_of(values, index, axis):
    share = values.shape[axis] // 2
    return lax.dynamic_slice_in_dim(values, index * share, share, axis)


def put_got(own, whole, got):
    return lax.dynamic_update_slice_in_dim(whole, got, (1 - own) * got.shape[0], 0)


def in_order(own, kept, got, axis):
    share = kept.shape[axis]
    shape = kept.shape[:axis] + (2 * share,) + kept.shape[axis + 1 :]
    both = lax.dynamic_update_slice_in_dim(jnp.zeros(shape, kept.dtype), kept, own * share, axis)
    return lax.dynamic_update_slice_in_dim(both, got, (1 - own) * share, axis)


def join(parts, axis):
    return parts[0] if len(parts) == 1 else jnp.concatenate(parts, axis)


class Term:
    def __init__(self, values, bits):
        self.values = values.reshape((2,) * len(bits) + values.shape[1:])
        self.bits = bits
        self.fixed = {}
        self.rows = (0, values.shape[1])
        self.columns = (0, values.shape[2])

    def narrowed(self, fixed=None, rows=None, columns=None):
        other = copy.copy(self)
        other.fixed = {**self.fixed, **(fixed or {})}
        if rows is not None:
            other.rows = (self.rows[0] + rows[0], rows[1])
        if columns is not None:
            other.columns = (self.columns[0] + columns[0], columns[1])
        return other

    def read(self):
        starts = [self.fixed.get(bit, 0) for bit in self.bits] + [self.rows[0], self.columns[0]]
        sizes = [1 if bit in self.fixed else 2 for bit in self.bits]
        left = math.prod(sizes)
        part = lax.dynamic_slice(self.values, starts, sizes + [self.rows[1], self.columns[1]])
        return part.reshape((left, self.rows[1], self.columns[1])).astype(F32)


class Shares:
    def __init__(self, shares, order):
        self.left = list(range(1, bits_of(lax.axis_size("dp"))))[::-1]
        self.order = [0] + order
        self.shares = shares
        self.by_column = False
        self.widths = []
        self.got = None
        self.parts = []

    def joined(self, narrow, axis):
        sums = [sum(term.narrowed(**narrow(term)).read() for term in terms) for terms in self.parts]
        return join([total.astype(BF16) for total in sums], axis)

    def keep(self, narrow):
        self.kept = self.joined(narrow, 2)

    def send(self):
        if not self.order or self.got is not None:
            return
        stage = self.order[0]
        own = lax.axis_index("blk")
        if stage == 0:
            self.got = [lax.ppermute(sent, "dp", flip("dp", 1)) for sent, _ in self.shares]
        elif stage == "last":
            self.kept = self.joined(lambda term: {}, 2)[0]
            self.got = swap_blk(self.kept)
        elif stage == "blk":

            def half(index):
                return lambda term: {
                    "columns": (index * (term.columns[1] // 2), term.columns[1] // 2)
                }

            self.widths = [terms[0].columns[1] // 2 for terms in self.parts]
            self.got = swap_blk(self.joined(half(1 - own), 2))
            self.keep(half(own))
        else:
            mine = (lax.axis_index("dp") >> stage) & 1
            sent = self.joined(lambda term: {"fixed": {stage: 1 - mine}}, 2)
            self.got = lax.ppermute(sent, "dp", flip("dp", 1 << stage))
            self.keep(lambda term: {"fixed": {stage: mine}})
            self.left = [bit for bit in self.left if bit != stage]

    def receive(self):
        stage = self.order.pop(0)
        got, self.got = self.got, None
        if stage == 0:
            self.parts = [
                [Term(kept, self.left), Term(new, self.left)]
                for (_, kept), new in zip(self.shares, got)
            ]
        elif stage == "last":
            if self.by_column:
                total = in_order(lax.axis_index("blk"), self.kept, got, 1).astype(F32)
                half = total.shape[1] // 2
                parts, start = [], 0
                for width in self.widths:
                    parts.append(total[:, start : start + width])
                    parts.append(total[:, half + start : half + start + width])
                    start += width
                self.total = jnp.concatenate(parts, axis=1)
            else:
                self.total = self.kept.astype(F32) + got.astype(F32)
        else:
            self.by_column = self.by_column or stage == "blk"
            self.parts = [[Term(self.kept, self.left), Term(got, self.left)]]

    def take_over(self, other):
        rows = self.parts[0][0].rows[1]
        for terms in other.parts:
            for start in range(0, terms[0].rows[1], rows):
                self.parts.append([term.narrowed(rows=(start, rows)) for term in terms])
                self.widths.append(terms[0].columns[1])


def receive(shares, *values):
    shares = [share for share in shares if share.got is not None]
    gots, values = lax.optimization_barrier(([share.got for share in shares], values))
    for share, got in zip(shares, gots):
        share.got = got
        share.receive()
    return values if len(values) > 1 else values[0]


def body(
    hidden,
    lengths,
    flags,
    buckets,
    g_attn,
    w_query,
    w_key,
    w_value,
    w_out,
    g_ffn,
    w_in,
    w_ffn_out,
    bias_table,
    cotangent,
):
    own = lax.axis_index("blk")
    size = lax.axis_size("dp")
    rest = list(range(1, bits_of(size)))
    first, second, later = rest[:1], rest[1:2], rest[2:]
    width = hidden.shape[2]
    seqs = hidden.shape[0] // 2
    count = hidden.shape[1] * 2
    tokens = seqs * count
    each = range(seqs)
    buckets_used, heads = bias_table.shape
    bias_width = 2 * count - LANES
    length = 2 * count

    with jax.named_scope("exchange_in"):
        def take(values, start, number):
            kept = lax.dynamic_slice_in_dim(values, own * seqs + start, number, 0)
            return kept, lax.dynamic_slice_in_dim(values, (1 - own) * seqs + start, number, 0)

        sent = lax.dynamic_slice_in_dim(hidden, (1 - own) * seqs, 1, 0)
        hidden_got = [swap_blk(sent)]
        hidden, cotangent, sent = lax.optimization_barrier((hidden, cotangent, sent))
        hidden_kept = [
            lax.dynamic_slice_in_dim(hidden, own * seqs + seq, 1, 0) for seq in each
        ]
        hidden_sent = [
            lax.dynamic_slice_in_dim(hidden, (1 - own) * seqs + seq, 1, 0) for seq in each
        ]
        early = 3 * count // 16
        upstream_kept = lax.dynamic_slice_in_dim(cotangent, own * seqs, seqs, 0)
        upstream_sent = lax.dynamic_slice_in_dim(cotangent, (1 - own) * seqs, seqs, 0)
        upstream_sent = [upstream_sent[:, :early], upstream_sent[:, early:]]
        valid_all = jnp.where(flags == 1, lengths[:, 1], lengths[:, 0])
        valid = lax.dynamic_slice_in_dim(valid_all, own * seqs, seqs, 0)
        scalars = jnp.stack([lax.axis_index("dp") & 1, own]).astype(jnp.int32)

    with jax.named_scope("bias"):
        w_all = jnp.stack([w_query, w_key, w_value])
        one_hot = (
            buckets[None, :] == jnp.arange(buckets_used, dtype=jnp.int32)[:, None]
        ).astype(F32)
        one_hot = jnp.pad(one_hot, ((0, 0), (0, length - buckets.shape[0])))
        vector = lax.dot_general(
            bias_table * LOG2E,
            one_hot,
            (((0,), (0,)), ((), ())),
            precision=lax.Precision.HIGHEST,
        )
        bias = expand_bias(jnp.roll(vector, -(LANES - 1), axis=1), bias_width)

    with jax.named_scope("exchange_in"):
        ready = (hidden_kept, hidden_sent, upstream_kept, upstream_sent, w_all, bias, valid, scalars)
        ready, hidden_got[0] = lax.optimization_barrier((ready, hidden_got[0]))
        hidden_kept, hidden_sent, upstream_kept, upstream_sent, w_all, bias, valid, scalars = ready
        hidden_got += [swap_blk(sent) for sent in hidden_sent[1:]]

    contexts, saved, hidden_seq, attn_in_seq = [], [], [], []
    for seq in each:
        with jax.named_scope("project"):
            kept, got = hidden_kept[seq], hidden_got[seq]
            if seq > 0:
                got, contexts[-1] = lax.optimization_barrier((got, contexts[-1]))
            if seq == seqs - 1:
                late, got = lax.optimization_barrier((upstream_sent[1], got))
                late = swap_blk(late)
            whole_seq, attn_in, projected = project(scalars, kept, got, g_attn, w_all)
            if seq == 0:
                first_part, projected = lax.optimization_barrier(
                    (upstream_sent[0], projected)
                )
                upstream_got = swap_blk(first_part)
            hidden_seq.append(whole_seq)
            attn_in_seq.append(attn_in)
        with jax.named_scope("attend"):
            context, *rest_of = attend(projected, bias, valid, seq)
            contexts.append(context)
            saved.append([projected, *rest_of])

    with jax.named_scope("middle"):
        inputs, late = lax.optimization_barrier((jnp.concatenate(hidden_seq, axis=0), late))
        upstream_got = jnp.concatenate([upstream_got, late], axis=1)
        upstream = in_order(own, upstream_kept, upstream_got, 1).reshape(tokens, width)
        act, grad_pre, ffn_in, output_kept, output_sent, grad_low, grad_context, *rest_of = middle(
            scalars, contexts, hidden_seq, upstream, w_out, g_ffn, w_in, w_ffn_out
        )
        sent, kept, grad_g_ffn = rest_of
    with jax.named_scope("output"):
        output_got = swap_blk(output_sent)

    with jax.named_scope("ffn_weights"):
        out_shares = Shares([out_weights(scalars, act, upstream)], first + ["blk"] + second)
        out_shares.send()
        in_sent, in_kept = in_weights(scalars, ffn_in, grad_pre)
        in_sent, in_kept = receive([out_shares], in_sent, in_kept)
        in_shares = Shares([(in_sent, in_kept)], second + first + ["blk"])
        in_shares.send()
        out_shares.send()
        grad_context = receive([in_shares], grad_context)
        in_shares.send()

    with jax.named_scope("attend_back"):
        pairs = width // LANES
        parting = 2 * pairs // 3
        weights = (w_query, w_key, w_value)
        bias_one, one_sent, one_kept, before = attend_back(
            scalars, saved, attn_in_seq, grad_context, weights, bias_width,
            (0, parting), None,
        )
        one_shares = Shares([(one_sent, one_kept), (sent, kept)], second + first + later + ["last"])
        one_shares.send()
        before, grad_context, output_got = receive(
            [out_shares, in_shares], before, grad_context, output_got
        )
        out_shares.send()
        in_shares.send()
        before, grad_context = receive([one_shares], before, grad_context)
        one_shares.send()
        bias_two, two_sent, two_kept, input_kept, input_sent, grad_g_attn = attend_back(
            scalars, saved, attn_in_seq, grad_context, weights, bias_width,
            (parting, pairs), (before, inputs, grad_low, g_attn),
        )
        two_shares = Shares([(two_sent, two_kept)], first + second + later + ["last"])
        two_shares.send()
        bias_one, bias_two, input_sent = receive(
            [one_shares, in_shares, out_shares], bias_one, bias_two, input_sent
        )

    with jax.named_scope("rounds"):
        for shares in (out_shares, in_shares, one_shares):
            shares.send()
        folded = fold_bias(bias_one, length), fold_bias(bias_two, length)
        *folded, input_sent = receive(
            [two_shares, one_shares, out_shares, in_shares], *folded, input_sent
        )
        in_shares.take_over(out_shares)
        in_shares.order = later + ["last"]
        input_got = swap_blk(input_sent)
        two_shares.send()
        in_shares.send()

    with jax.named_scope("small"):
        table = lax.dot_general(
            one_hot,
            jnp.concatenate(folded, axis=0),
            (((1,), (1,)), ((), ())),
            precision=lax.Precision.HIGHEST,
        )
        flat = jnp.concatenate([grad_g_attn[0], grad_g_ffn[0], table.reshape(-1)])
        flat = jnp.pad(flat, (0, -flat.shape[0] % 1024)).reshape(-1, LANES)
        if size > 1:
            flat = flat + lax.ppermute(flat, "dp", flip("dp", 1))
        small_bits = list(range(1, bits_of(size))) + ["blk"]

    def small_step(flat, chains, *others):
        if not small_bits:
            flat, *others = receive(chains, flat, *others, 0)[:-1]
            return flat, *others
        bit = small_bits.pop(0)
        got = swap_blk(flat) if bit == "blk" else lax.ppermute(flat, "dp", flip("dp", 1 << bit))
        flat, got, *others = receive(chains, flat, got, *others)
        return flat + got, *others

    with jax.named_scope("rounds"):
        one_shares.send()
        (flat,) = small_step(flat, [two_shares])
        two_shares.send()
        flat, input_got = small_step(flat, [two_shares, in_shares], input_got)
        chains = [two_shares, one_shares, in_shares]
        while any(shares.order for shares in chains) or small_bits:
            for shares in chains:
                shares.send()
            (flat,) = small_step(flat, chains)

    one, two = one_shares.total, two_shares.total
    pieces = jnp.split(one[:, : 3 * LANES * parting], 3 * parting, axis=1)
    pieces += jnp.split(two, 3 * (pairs - parting), axis=1)
    grad_query_w, grad_key_w, grad_value_w = (
        jnp.concatenate(pieces[part::3], axis=1) for part in range(3)
    )
    grad_out_w = one[:, 3 * LANES * parting :]
    two = in_shares.total
    units = w_in.shape[1]
    grad_in = two[:, :units]
    grad_ffn_out = jnp.concatenate(
        [two[:, start : start + width] for start in range(units, two.shape[1], width)], axis=0
    )
    with jax.named_scope("output"):
        output = put_got(own, output_kept, output_got)
        input_grad = put_got(own, input_kept, input_got)

    with jax.named_scope("small"):
        flat = flat.reshape(-1)
        share = width // size
        at = lax.axis_index("dp") * share
        gain_attn = lax.dynamic_slice_in_dim(flat[:width], at, share)
        gain_ffn = lax.dynamic_slice_in_dim(flat[width : 2 * width], at, share)
        table = flat[2 * width : 2 * width + buckets_used * heads].reshape(buckets_used, heads)

    return (
        output,
        input_grad,
        gain_attn,
        grad_query_w,
        grad_key_w,
        grad_value_w,
        grad_out_w,
        gain_ffn,
        grad_in,
        grad_ffn_out,
        table,
    )


def solution(mesh):
    split = P("dp", "blk", None)
    rows = P("dp", None)
    in_specs = (split, rows, P("dp")) + (P(),) * 10 + (split,)
    out_specs = (split, split, P("dp")) + (rows,) * 4 + (P("dp"), rows, rows, P())
    return jax.shard_map(body, mesh=mesh, in_specs=in_specs, out_specs=out_specs, check_vma=False)
```

profile of v0, /device:TPU:0, one launch (start us, length us, event | category | flops | bytes accessed | tf_op | source)
XLA Modules:
  0.0 224.4 jit_solution(2811903011359686953)
XLA Ops:
  0.7 1.9 constant_dynamic-slice_fusion.10
  2.6 2.9 %collective-permute-start = (bf16[1,256,768]{2,1,0:T(8,128)(2,1)}, bf16[1,256,768]{2,1,0:T(8,128)(2,1)S(1)}, u32[]{:S(2)}, u32[]{:S(2)}) collective-permute-start(bf16[1,256,768]{2,1,0:T(8,128)(2,1)} %constant_dynamic-slice_fusion.10), channel_id=1, source_target_pairs={{0,1},{1,0},{2,3},{3,2},{4,5},{5,4},{6,7},{7,6},{8,9},{9,8},{10,11... | collective-permute-start | bytes 1179656 | tf_op jit(solution)/shard_map/exchange_in/ppermute | solution.py:680
  9.7 1.9 bias.1.bias_ref
  11.6 2.4 %copy-done.4 = f32[12,128,896]{2,1,0:T(8,128)} copy-done((f32[12,128,896]{2,1,0:T(8,128)}, f32[12,128,896]{2,1,0:T(8,128)S(1)}, u32[]{:S(2)}) %copy-start.4) | copy-done | bytes 5505048
  16.0 1.6 pad_maximum_fusion.w_ref
  17.7 3.3 %project.2 = (bf16[512,768]{1,0:T(8,128)(2,1)S(1)}, bf16[512,768]{1,0:T(8,128)(2,1)S(1)}, bf16[3,512,768]{2,1,0:T(8,128)(2,1)S(1)}) custom-call(s32[2]{0:T(128)S(1)} %pad_add_fusion.scalars, bf16[1,256,768]{2,1,0:T(8,128)(2,1)S(1)} %get-tuple-element.120.kept_ref, bf16[1,256,768]{2,1,0:T(8,128)(2,1)S(1)} %collective-permute-done.got_ref, ...), custom_call_target="tpu_custom_call" | custom-call | flops 1811939328 | bytes 8388608 | tf_op jit(solution)/shard_map/project/pallas_call | solution.py:119
  21.1 2.0 collective-permute-start.2
  23.4 7.7 %attend.2 = (bf16[512,768]{1,0:T(8,128)(2,1)S(1)}, bf16[512,768]{1,0:T(8,128)(2,1)}, bf16[12,512,512]{2,1,0:T(8,128)(2,1)}, f32[512,768]{1,0:T(8,128)}) custom-call(s32[2]{0:T(128)S(1)} %dynamic_slice.214.valid, bf16[3,512,768]{2,1,0:T(8,128)(2,1)S(1)} %get-tuple-element.124.q_ref.k_ref.v_ref.refs_0_.refs_1_.refs_2_, ...), custom_call_target="tpu_custom_call" | custom-call | flops 6442450944 | bytes 12582912 | tf_op jit(solution)/shard_map/attend/pallas_call | solution.py:213
  31.1 2.1 collective-permute-done.1.got_ref
  33.1 3.3 %project.3 = (bf16[512,768]{1,0:T(8,128)(2,1)S(1)}, bf16[512,768]{1,0:T(8,128)(2,1)S(1)}, bf16[3,512,768]{2,1,0:T(8,128)(2,1)S(1)}) custom-call(s32[2]{0:T(128)S(1)} %pad_add_fusion.scalars, bf16[1,256,768]{2,1,0:T(8,128)(2,1)S(1)} %get-tuple-element.128.kept_ref, bf16[1,256,768]{2,1,0:T(8,128)(2,1)S(1)} %collective-permute-done.1.got_ref, ...), custom_call_target="tpu_custom_call" | custom-call | flops 1811939328 | bytes 8388608 | tf_op jit(solution)/shard_map/project/pallas_call | solution.py:119
  36.5 7.8 %attend.3 = (bf16[512,768]{1,0:T(8,128)(2,1)S(1)}, bf16[512,768]{1,0:T(8,128)(2,1)}, bf16[12,512,512]{2,1,0:T(8,128)(2,1)}, f32[512,768]{1,0:T(8,128)}) custom-call(s32[2]{0:T(128)S(1)} %dynamic_slice.214.valid, bf16[3,512,768]{2,1,0:T(8,128)(2,1)S(1)} %get-tuple-element.132.q_ref.k_ref.v_ref.refs_3_.refs_4_.refs_5_, ...), custom_call_target="tpu_custom_call" | custom-call | flops 6442450944 | bytes 12582912 | tf_op jit(solution)/shard_map/attend/pallas_call | solution.py:213
  45.6 2.9 %collective-permute-done.3 = bf16[2,160,768]{2,1,0:T(8,128)(2,1)S(1)} collective-permute-done((bf16[2,160,768]{2,1,0:T(8,128)(2,1)S(1)}, bf16[2,160,768]{2,1,0:T(8,128)(2,1)S(1)}, u32[]{:S(2)}, u32[]{:S(2)}) %collective-permute-start.3) | collective-permute-done | bytes 491552 | tf_op jit(solution)/shard_map/project/ppermute | solution.py:680
  48.6 33.8 %middle.1 = (bf16[1024,3072]{1,0:T(8,128)(2,1)S(1)}, bf16[1024,3072]{1,0:T(8,128)(2,1)S(1)}, bf16[1024,768]{1,0:T(8,128)(2,1)S(1)}, bf16[4,256,768]{2,1,0:T(8,12...) custom-call(s32[2]{0:T(128)S(1)} %pad_add_fusion.scalars, ...), custom_call_target="tpu_custom_call" | custom-call | flops 19327352832 | bytes 20971520 | tf_op jit(solution)/shard_map/middle/pallas_call | solution.py:627
  82.4 7.6 %ffn_weights.2 = (bf16[8,48,3072]{2,1,0:T(8,128)(2,1)}, bf16[8,48,3072]{2,1,0:T(8,128)(2,1)}) custom-call(s32[2]{0:T(128)S(1)} %pad_add_fusion.scalars, bf16[1024,3072]{1,0:T(8,128)(2,1)S(1)} %get-tuple-element.141.act_ref, bf16[1024,768]{1,0:T(8,128)(2,1)S(1)} %bitcast.128), custom_call_target="tpu_custom_call" | custom-call | tf_op jit(solution)/shard_map/ffn_weights/pallas_call | solution.py:524
  90.0 7.5 %ffn_weights.3 = (bf16[8,48,3072]{2,1,0:T(8,128)(2,1)}, bf16[8,48,3072]{2,1,0:T(8,128)(2,1)}) custom-call(s32[2]{0:T(128)S(1)} %pad_add_fusion.scalars, bf16[1024,768]{1,0:T(8,128)(2,1)S(1)} %get-tuple-element.144.ffn_in_ref, bf16[1024,3072]{1,0:T(8,128)(2,1)S(1)} %get-tuple-element.145.pre_ref), custom_call_target="tpu_custom_call" | custom-call | tf_op jit(solution)/shard_map/ffn_weights/pallas_call | solution.py:497
  98.3 2.2 add_convert_fusion.3
  100.5 1.8 collective-permute-start.5
  103.2 1.8 add_convert_fusion.2
  106.0 1.7 add_convert_fusion
  107.7 22.8 %attend_back.2 = (f32[8,128,896]{2,1,0:T(8,128)}, bf16[8,48,1536]{2,1,0:T(8,128)(2,1)}, bf16[8,48,1536]{2,1,0:T(8,128)(2,1)}, bf16[1024,768]{1,0:T(8,128)(2,1)}) custom-call(s32[2]{0:T(128)S(1)} %pad_add_fusion.scalars, bf16[3,512,768]{2,1,0:T(8,128)(2,1)} %copy-done.2, bf16[3,512,768]{2,1,0:T(8,128)(2,1)} %copy-done.2, bf16[3,512,768]{2,1,0:T(8,128)(2,1)} %copy-done.2, ...), custom_call_target="tpu_custom_call" | custom-call | tf_op jit(solution)/shard_map/attend_back/pallas_call | solution.py:465
  137.8 17.6 %attend_back.3 = (f32[4,128,896]{2,1,0:T(8,128)}, bf16[8,48,768]{2,1,0:T(8,128)(2,1)}, bf16[8,48,768]{2,1,0:T(8,128)(2,1)}, bf16[4,256,768]{2,1,0:T(8,128)(2,1)}...) custom-call(s32[2]{0:T(128)S(1)} %pad_add_fusion.scalars, bf16[3,512,768]{2,1,0:T(8,128)(2,1)} %copy-done.2, ...), custom_call_target="tpu_custom_call" | custom-call | tf_op jit(solution)/shard_map/attend_back/pallas_call | solution.py:465
  162.3 3.6 %rounds.2 = f32[8,8,1024]{2,1,0:T(8,128)S(1)} custom-call(f32[8,128,896]{2,1,0:T(8,128)} %get-tuple-element.188.grad_ref), custom_call_target="tpu_custom_call" | custom-call | tf_op jit(solution)/shard_map/rounds/pallas_call | solution.py:80
  166.0 2.6 %rounds.3 = f32[4,8,1024]{2,1,0:T(8,128)S(1)} custom-call(f32[4,128,896]{2,1,0:T(8,128)} %get-tuple-element.189.grad_ref), custom_call_target="tpu_custom_call" | custom-call | tf_op jit(solution)/shard_map/rounds/pallas_call | solution.py:80
  169.4 2.0 collective-permute-done.15
  176.0 2.6 %collective-permute-start.22 = (bf16[1,48,3072]{2,1,0:T(8,128)(2,1)S(1)}, bf16[1,48,3072]{2,1,0:T(8,128)(2,1)S(1)}, u32[]{:S(2)}, u32[]{:S(2)}) collective-permute-start(bf16[1,48,3072]{2,1,0:T(8,128)(2,1)S(1)} %pad_maximum_fusion.5), channel_id=1, source_target_pairs={{0,16},{2,18},{4,20},{6,22},{8,24},{10,26},{12,28},{14,30},{16,0},... | collective-permute-start | bytes 884744 | tf_op jit(solution)/shard_map/rounds/ppermute | solution.py:772
  180.8 1.7 collective-permute-done.20
  185.6 6.6 %collective-permute-done.22 = bf16[1,48,3072]{2,1,0:T(8,128)(2,1)S(1)} collective-permute-done((bf16[1,48,3072]{2,1,0:T(8,128)(2,1)S(1)}, bf16[1,48,3072]{2,1,0:T(8,128)(2,1)S(1)}, u32[]{:S(2)}, u32[]{:S(2)}) %collective-permute-start.22) | collective-permute-done | bytes 294944 | tf_op jit(solution)/shard_map/rounds/ppermute | solution.py:772
  192.2 2.4 %collective-permute-done.23 = f32[16,128]{1,0:T(8,128)S(1)} collective-permute-done((f32[16,128]{1,0:T(8,128)S(1)}, f32[16,128]{1,0:T(8,128)S(1)}, u32[]{:S(2)}, u32[]{:S(2)}) %collective-permute-start.23) | collective-permute-done | bytes 8224 | tf_op jit(solution)/shard_map/rounds/ppermute | solution.py:990
  195.2 2.4 %collective-permute-start.26 = (bf16[1,48,2304]{2,1,0:T(8,128)(2,1)S(1)}, bf16[1,48,2304]{2,1,0:T(8,128)(2,1)S(1)}, u32[]{:S(2)}, u32[]{:S(2)}) collective-permute-start(bf16[1,48,2304]{2,1,0:T(8,128)(2,1)S(1)} %fusion.12), channel_id=1, source_target_pairs={{0,16},{2,18},{4,20},{6,22},{8,24},{10,26},{12,28},{14,30},{16,0},... | collective-permute-start | bytes 663560 | tf_op jit(solution)/shard_map/rounds/ppermute | solution.py:772
  198.3 2.4 %collective-permute-start.25 = (bf16[1,48,768]{2,1,0:T(8,128)(2,1)S(1)}, bf16[1,48,768]{2,1,0:T(8,128)(2,1)S(1)}, u32[]{:S(2)}, u32[]{:S(2)}) collective-permute-start(bf16[1,48,768]{2,1,0:T(8,128)(2,1)S(1)} %fusion.22), channel_id=1, source_target_pairs={{0,16},{2,18},{4,20},{6,22},{8,24},{10,26},{12,28},{14,30},{16,0},... | collective-permute-start | bytes 221192 | tf_op jit(solution)/shard_map/rounds/ppermute | solution.py:772
  201.9 7.1 %collective-permute-done.26 = bf16[1,48,2304]{2,1,0:T(8,128)(2,1)S(1)} collective-permute-done((bf16[1,48,2304]{2,1,0:T(8,128)(2,1)S(1)}, bf16[1,48,2304]{2,1,0:T(8,128)(2,1)S(1)}, u32[]{:S(2)}, u32[]{:S(2)}) %collective-permute-start.26) | collective-permute-done | bytes 221216 | tf_op jit(solution)/shard_map/rounds/ppermute | solution.py:772
  216.0 4.8 %collective-permute-done.29 = bf16[48,768]{1,0:T(8,128)(2,1)S(1)} collective-permute-done((bf16[48,768]{1,0:T(8,128)(2,1)S(1)}, bf16[48,768]{1,0:T(8,128)(2,1)S(1)}, u32[]{:S(2)}, u32[]{:S(2)}) %collective-permute-start.29) | collective-permute-done | bytes 73760 | tf_op jit(solution)/shard_map/rounds/ppermute | solution.py:680
  (192 shorter events, 48.0 us)
Async XLA Ops:
  2.6 15.1 %collective-permute-start = (bf16[1,256,768]{2,1,0:T(8,128)(2,1)}, bf16[1,256,768]{2,1,0:T(8,128)(2,1)S(1)}, u32[]{:S(2)}, u32[]{:S(2)}) collective-permute-start(bf16[1,256,768]{2,1,0:T(8,128)(2,1)} %constant_dynamic-slice_fusion.10), channel_id=1, source_target_pairs={{0,1},{1,0},{2,3},{3,2},{4,5},{5,4},{6,7},{7,6},{8,9},{9,8},{10,11... | collective-permute-start | bytes 1179656 | tf_op jit(solution)/shard_map/exchange_in/ppermute | solution.py:680
  21.0 12.1 %collective-permute-start.1 = (bf16[1,256,768]{2,1,0:T(8,128)(2,1)S(1)}, bf16[1,256,768]{2,1,0:T(8,128)(2,1)S(1)}, u32[]{:S(2)}, u32[]{:S(2)}) collective-permute-start(bf16[1,256,768]{2,1,0:T(8,128)(2,1)S(1)} %get-tuple-element.117), channel_id=1, source_target_pairs={{0,1},{1,0},{2,3},{3,2},{4,5},{5,4},{6,7},{7,6},{8,9},{9,8},{10,11... | collective-permute-start | bytes 1179656 | tf_op jit(solution)/shard_map/exchange_in/ppermute | solution.py:680
  21.1 27.4 %collective-permute-start.2 = (bf16[2,96,768]{2,1,0:T(8,128)(2,1)S(1)}, bf16[2,96,768]{2,1,0:T(8,128)(2,1)S(1)}, u32[]{:S(2)}, u32[]{:S(2)}) collective-permute-start(bf16[2,96,768]{2,1,0:T(8,128)(2,1)S(1)} %copy-done.15), channel_id=1, source_target_pairs={{0,1},{1,0},{2,3},{3,2},{4,5},{5,4},{6,7},{7,6},{8,9},{9,8},{10,11... | collective-permute-start | bytes 884744 | tf_op jit(solution)/shard_map/project/ppermute | solution.py:680
  33.1 15.4 %collective-permute-start.3 = (bf16[2,160,768]{2,1,0:T(8,128)(2,1)S(1)}, bf16[2,160,768]{2,1,0:T(8,128)(2,1)S(1)}, u32[]{:S(2)}, u32[]{:S(2)}) collective-permute-start(bf16[2,160,768]{2,1,0:T(8,128)(2,1)S(1)} %copy-done.14), channel_id=1, source_target_pairs={{0,1},{1,0},{2,3},{3,2},{4,5},{5,4},{6,7},{7,6},{8,9},{9,8},{10,11... | collective-permute-start | bytes 1474568 | tf_op jit(solution)/shard_map/project/ppermute | solution.py:680
  90.0 7.5 %collective-permute-start.4 = (bf16[8,48,3072]{2,1,0:T(8,128)(2,1)}, bf16[8,48,3072]{2,1,0:T(8,128)(2,1)}, u32[]{:S(2)}, u32[]{:S(2)}) collective-permute-start(bf16[8,48,3072]{2,1,0:T(8,128)(2,1)} %get-tuple-element.143), channel_id=1, source_target_pairs={{0,2},{2,0},{4,6},{6,4},{8,10},{10,8},{12,14},{14,12},{16,18},{18,... | collective-permute-start | bytes 7077896 | tf_op jit(solution)/shard_map/ffn_weights/ppermute | solution.py:755
  97.5 5.6 %collective-permute-start.6 = (bf16[8,48,3072]{2,1,0:T(8,128)(2,1)}, bf16[8,48,3072]{2,1,0:T(8,128)(2,1)}, u32[]{:S(2)}, u32[]{:S(2)}) collective-permute-start(bf16[8,48,3072]{2,1,0:T(8,128)(2,1)} %get-tuple-element.150), channel_id=1, source_target_pairs={{0,2},{2,0},{4,6},{6,4},{8,10},{10,8},{12,14},{14,12},{16,18},{18,... | collective-permute-start | bytes 7077896 | tf_op jit(solution)/shard_map/ffn_weights/ppermute | solution.py:755
  98.0 34.5 %collective-permute-start.8 = (bf16[2,256,768]{2,1,0:T(8,128)(2,1)S(1)}, bf16[2,256,768]{2,1,0:T(8,128)(2,1)S(1)}, u32[]{:S(2)}, u32[]{:S(2)}) collective-permute-start(bf16[2,256,768]{2,1,0:T(8,128)(2,1)S(1)} %copy-done.28), channel_id=1, source_target_pairs={{0,1},{1,0},{2,3},{3,2},{4,5},{5,4},{6,7},{7,6},{8,9},{9,8},{10,11... | collective-permute-start | bytes 2359304 | tf_op jit(solution)/shard_map/output/ppermute | solution.py:680
  98.3 36.0 %collective-permute-start.10 = (bf16[8,48,768]{2,1,0:T(8,128)(2,1)}, bf16[8,48,768]{2,1,0:T(8,128)(2,1)S(1)}, u32[]{:S(2)}, u32[]{:S(2)}) collective-permute-start(bf16[8,48,768]{2,1,0:T(8,128)(2,1)} %get-tuple-element.166), channel_id=1, source_target_pairs={{0,2},{2,0},{4,6},{6,4},{8,10},{10,8},{12,14},{14,12},{16,18},{18,... | collective-permute-start | bytes 1769480 | tf_op jit(solution)/shard_map/attend_back/ppermute | solution.py:755
  100.5 32.0 %collective-permute-start.5 = (bf16[4,48,3072]{2,1,0:T(8,128)(2,1)S(1)}, bf16[4,48,3072]{2,1,0:T(8,128)(2,1)S(1)}, u32[]{:S(2)}, u32[]{:S(2)}) collective-permute-start(bf16[4,48,3072]{2,1,0:T(8,128)(2,1)S(1)} %bitcast.148), channel_id=1, source_target_pairs={{0,4},{2,6},{4,0},{6,2},{8,12},{10,14},{12,8},{14,10},{16,20},{18,... | collective-permute-start | bytes 3538952 | tf_op jit(solution)/shard_map/ffn_weights/ppermute | solution.py:772
  105.0 28.3 %collective-permute-start.7 = (bf16[4,48,3072]{2,1,0:T(8,128)(2,1)S(1)}, bf16[4,48,3072]{2,1,0:T(8,128)(2,1)S(1)}, u32[]{:S(2)}, u32[]{:S(2)}) collective-permute-start(bf16[4,48,3072]{2,1,0:T(8,128)(2,1)S(1)} %bitcast.149), channel_id=1, source_target_pairs={{0,8},{2,10},{4,12},{6,14},{8,0},{10,2},{12,4},{14,6},{16,24},{18,... | collective-permute-start | bytes 3538952 | tf_op jit(solution)/shard_map/ffn_weights/ppermute | solution.py:772
  130.5 3.8 %collective-permute-start.9 = (bf16[8,48,1536]{2,1,0:T(8,128)(2,1)}, bf16[8,48,1536]{2,1,0:T(8,128)(2,1)S(1)}, u32[]{:S(2)}, u32[]{:S(2)}) collective-permute-start(bf16[8,48,1536]{2,1,0:T(8,128)(2,1)} %get-tuple-element.165), channel_id=1, source_target_pairs={{0,2},{2,0},{4,6},{6,4},{8,10},{10,8},{12,14},{14,12},{16,18},{18,... | collective-permute-start | bytes 3538952 | tf_op jit(solution)/shard_map/attend_back/ppermute | solution.py:755
  133.7 22.1 %collective-permute-start.14 = (bf16[4,48,1536]{2,1,0:T(8,128)(2,1)S(1)}, bf16[4,48,1536]{2,1,0:T(8,128)(2,1)S(1)}, u32[]{:S(2)}, u32[]{:S(2)}) collective-permute-start(bf16[4,48,1536]{2,1,0:T(8,128)(2,1)S(1)} %bitcast.158), channel_id=1, source_target_pairs={{0,1},{1,0},{2,3},{3,2},{4,5},{5,4},{6,7},{7,6},{8,9},{9,8},{10,11... | collective-permute-start | bytes 1769480 | tf_op jit(solution)/shard_map/attend_back/ppermute | solution.py:680
  135.0 21.4 %collective-permute-start.12 = (bf16[4,48,2304]{2,1,0:T(8,128)(2,1)S(1)}, bf16[4,48,2304]{2,1,0:T(8,128)(2,1)S(1)}, u32[]{:S(2)}, u32[]{:S(2)}) collective-permute-start(bf16[4,48,2304]{2,1,0:T(8,128)(2,1)S(1)} %pad_maximum_fusion.2), channel_id=1, source_target_pairs={{0,8},{2,10},{4,12},{6,14},{8,0},{10,2},{12,4},{14,6},{16,24},{18,... | collective-permute-start | bytes 2654216 | tf_op jit(solution)/shard_map/attend_back/ppermute | solution.py:772
  136.4 19.4 %collective-permute-start.13 = (bf16[2,48,3072]{2,1,0:T(8,128)(2,1)S(1)}, bf16[2,48,3072]{2,1,0:T(8,128)(2,1)S(1)}, u32[]{:S(2)}, u32[]{:S(2)}) collective-permute-start(bf16[2,48,3072]{2,1,0:T(8,128)(2,1)S(1)} %fusion.5), channel_id=1, source_target_pairs={{0,4},{2,6},{4,0},{6,2},{8,12},{10,14},{12,8},{14,10},{16,20},{18,... | collective-permute-start | bytes 1769480 | tf_op jit(solution)/shard_map/attend_back/ppermute | solution.py:772
  155.3 13.3 %collective-permute-start.11 = (bf16[8,48,768]{2,1,0:T(8,128)(2,1)}, bf16[8,48,768]{2,1,0:T(8,128)(2,1)}, u32[]{:S(2)}, u32[]{:S(2)}) collective-permute-start(bf16[8,48,768]{2,1,0:T(8,128)(2,1)} %get-tuple-element.175), channel_id=1, source_target_pairs={{0,2},{2,0},{4,6},{6,4},{8,10},{10,8},{12,14},{14,12},{16,18},{18,... | collective-permute-start | bytes 1769480 | tf_op jit(solution)/shard_map/attend_back/ppermute | solution.py:755
  157.3 11.3 %collective-permute-start.17 = (bf16[2,48,1536]{2,1,0:T(8,128)(2,1)}, bf16[2,48,1536]{2,1,0:T(8,128)(2,1)S(1)}, u32[]{:S(2)}, u32[]{:S(2)}) collective-permute-start(bf16[2,48,1536]{2,1,0:T(8,128)(2,1)} %get-tuple-element.252), channel_id=1, source_target_pairs={{0,1},{1,0},{2,3},{3,2},{4,5},{5,4},{6,7},{7,6},{8,9},{9,8},{10,11... | collective-permute-start | bytes 884744 | tf_op jit(solution)/shard_map/rounds/ppermute | solution.py:680
  159.5 11.9 %collective-permute-start.15 = (bf16[2,48,2304]{2,1,0:T(8,128)(2,1)}, bf16[2,48,2304]{2,1,0:T(8,128)(2,1)S(1)}, u32[]{:S(2)}, u32[]{:S(2)}) collective-permute-start(bf16[2,48,2304]{2,1,0:T(8,128)(2,1)} %get-tuple-element.233), channel_id=1, source_target_pairs={{0,4},{2,6},{4,0},{6,2},{8,12},{10,14},{12,8},{14,10},{16,20},{18,... | collective-permute-start | bytes 1327112 | tf_op jit(solution)/shard_map/rounds/ppermute | solution.py:772
  161.5 7.9 %collective-permute-start.16 = (bf16[2,48,1536]{2,1,0:T(8,128)(2,1)}, bf16[2,48,1536]{2,1,0:T(8,128)(2,1)S(1)}, u32[]{:S(2)}, u32[]{:S(2)}) collective-permute-start(bf16[2,48,1536]{2,1,0:T(8,128)(2,1)} %get-tuple-element.238), channel_id=1, source_target_pairs={{0,8},{2,10},{4,12},{6,14},{8,0},{10,2},{12,4},{14,6},{16,24},{18,... | collective-permute-start | bytes 884744 | tf_op jit(solution)/shard_map/rounds/ppermute | solution.py:772
  171.7 6.9 %collective-permute-start.19 = (f32[16,128]{1,0:T(8,128)S(1)}, f32[16,128]{1,0:T(8,128)S(1)}, u32[]{:S(2)}, u32[]{:S(2)}) collective-permute-start(f32[16,128]{1,0:T(8,128)S(1)} %fusion.32), channel_id=1, source_target_pairs={{0,2},{2,0},{4,6},{6,4},{8,10},{10,8},{12,14},{14,12},{16,18},{18,... | collective-permute-start | bytes 24584 | tf_op jit(solution)/shard_map/small/ppermute | solution.py:982
  172.9 9.6 %collective-permute-start.18 = (bf16[4,48,768]{2,1,0:T(8,128)(2,1)S(1)}, bf16[4,48,768]{2,1,0:T(8,128)(2,1)S(1)}, u32[]{:S(2)}, u32[]{:S(2)}) collective-permute-start(bf16[4,48,768]{2,1,0:T(8,128)(2,1)S(1)} %bitcast.159), channel_id=1, source_target_pairs={{0,4},{2,6},{4,0},{6,2},{8,12},{10,14},{12,8},{14,10},{16,20},{18,... | collective-permute-start | bytes 884744 | tf_op jit(solution)/shard_map/rounds/ppermute | solution.py:772
  173.4 21.1 %collective-permute-start.24 = (bf16[2,256,768]{2,1,0:T(8,128)(2,1)}, bf16[2,256,768]{2,1,0:T(8,128)(2,1)}, u32[]{:S(2)}, u32[]{:S(2)}) collective-permute-start(bf16[2,256,768]{2,1,0:T(8,128)(2,1)} %get-tuple-element.201), channel_id=1, source_target_pairs={{0,1},{1,0},{2,3},{3,2},{4,5},{5,4},{6,7},{7,6},{8,9},{9,8},{10,11... | collective-permute-start | bytes 2359304 | tf_op jit(solution)/shard_map/rounds/ppermute | solution.py:680
  176.0 16.2 %collective-permute-start.22 = (bf16[1,48,3072]{2,1,0:T(8,128)(2,1)S(1)}, bf16[1,48,3072]{2,1,0:T(8,128)(2,1)S(1)}, u32[]{:S(2)}, u32[]{:S(2)}) collective-permute-start(bf16[1,48,3072]{2,1,0:T(8,128)(2,1)S(1)} %pad_maximum_fusion.5), channel_id=1, source_target_pairs={{0,16},{2,18},{4,20},{6,22},{8,24},{10,26},{12,28},{14,30},{16,0},... | collective-permute-start | bytes 884744 | tf_op jit(solution)/shard_map/rounds/ppermute | solution.py:772
  178.6 3.8 %collective-permute-start.20 = (f32[16,128]{1,0:T(8,128)S(1)}, f32[16,128]{1,0:T(8,128)S(1)}, u32[]{:S(2)}, u32[]{:S(2)}) collective-permute-start(f32[16,128]{1,0:T(8,128)S(1)} %fusion.42), channel_id=1, source_target_pairs={{0,4},{2,6},{4,0},{6,2},{8,12},{10,14},{12,8},{14,10},{16,20},{18,... | collective-permute-start | bytes 24584 | tf_op jit(solution)/shard_map/rounds/ppermute | solution.py:990
  182.6 12.0 %collective-permute-start.21 = (bf16[2,48,768]{2,1,0:T(8,128)(2,1)S(1)}, bf16[2,48,768]{2,1,0:T(8,128)(2,1)S(1)}, u32[]{:S(2)}, u32[]{:S(2)}) collective-permute-start(bf16[2,48,768]{2,1,0:T(8,128)(2,1)S(1)} %get-tuple-element.250), channel_id=1, source_target_pairs={{0,8},{2,10},{4,12},{6,14},{8,0},{10,2},{12,4},{14,6},{16,24},{18,... | collective-permute-start | bytes 442376 | tf_op jit(solution)/shard_map/rounds/ppermute | solution.py:772
  183.1 11.5 %collective-permute-start.23 = (f32[16,128]{1,0:T(8,128)S(1)}, f32[16,128]{1,0:T(8,128)S(1)}, u32[]{:S(2)}, u32[]{:S(2)}) collective-permute-start(f32[16,128]{1,0:T(8,128)S(1)} %add.308), channel_id=1, source_target_pairs={{0,8},{2,10},{4,12},{6,14},{8,0},{10,2},{12,4},{14,6},{16,24},{18,... | collective-permute-start | bytes 24584 | tf_op jit(solution)/shard_map/rounds/ppermute | solution.py:990
  194.7 16.0 %collective-permute-start.27 = (bf16[48,3072]{1,0:T(8,128)(2,1)S(1)}, bf16[48,3072]{1,0:T(8,128)(2,1)S(1)}, u32[]{:S(2)}, u32[]{:S(2)}) collective-permute-start(bf16[48,3072]{1,0:T(8,128)(2,1)S(1)} %get-tuple-element.229), channel_id=1, source_target_pairs={{0,1},{1,0},{2,3},{3,2},{4,5},{5,4},{6,7},{7,6},{8,9},{9,8},{10,11... | collective-permute-start | bytes 884744 | tf_op jit(solution)/shard_map/rounds/ppermute | solution.py:680
  195.2 13.8 %collective-permute-start.26 = (bf16[1,48,2304]{2,1,0:T(8,128)(2,1)S(1)}, bf16[1,48,2304]{2,1,0:T(8,128)(2,1)S(1)}, u32[]{:S(2)}, u32[]{:S(2)}) collective-permute-start(bf16[1,48,2304]{2,1,0:T(8,128)(2,1)S(1)} %fusion.12), channel_id=1, source_target_pairs={{0,16},{2,18},{4,20},{6,22},{8,24},{10,26},{12,28},{14,30},{16,0},... | collective-permute-start | bytes 663560 | tf_op jit(solution)/shard_map/rounds/ppermute | solution.py:772
  197.7 11.5 %collective-permute-start.28 = (f32[16,128]{1,0:T(8,128)S(1)}, f32[16,128]{1,0:T(8,128)S(1)}, u32[]{:S(2)}, u32[]{:S(2)}) collective-permute-start(f32[16,128]{1,0:T(8,128)S(1)} %add.318), channel_id=1, source_target_pairs={{0,16},{2,18},{4,20},{6,22},{8,24},{10,26},{12,28},{14,30},{16,0},... | collective-permute-start | bytes 24584 | tf_op jit(solution)/shard_map/rounds/ppermute | solution.py:990
  198.3 12.4 %collective-permute-start.25 = (bf16[1,48,768]{2,1,0:T(8,128)(2,1)S(1)}, bf16[1,48,768]{2,1,0:T(8,128)(2,1)S(1)}, u32[]{:S(2)}, u32[]{:S(2)}) collective-permute-start(bf16[1,48,768]{2,1,0:T(8,128)(2,1)S(1)} %fusion.22), channel_id=1, source_target_pairs={{0,16},{2,18},{4,20},{6,22},{8,24},{10,26},{12,28},{14,30},{16,0},... | collective-permute-start | bytes 221192 | tf_op jit(solution)/shard_map/rounds/ppermute | solution.py:772
  210.8 5.3 %collective-permute-start.31 = (f32[16,128]{1,0:T(8,128)S(1)}, f32[16,128]{1,0:T(8,128)S(1)}, u32[]{:S(2)}, u32[]{:S(2)}) collective-permute-start(f32[16,128]{1,0:T(8,128)S(1)} %add.322), channel_id=1, source_target_pairs={{0,1},{1,0},{2,3},{3,2},{4,5},{5,4},{6,7},{7,6},{8,9},{9,8},{10,11... | collective-permute-start | bytes 24584 | tf_op jit(solution)/shard_map/rounds/ppermute | solution.py:680
  212.1 8.7 %collective-permute-start.30 = (bf16[48,2304]{1,0:T(8,128)(2,1)S(1)}, bf16[48,2304]{1,0:T(8,128)(2,1)S(1)}, u32[]{:S(2)}, u32[]{:S(2)}) collective-permute-start(bf16[48,2304]{1,0:T(8,128)(2,1)S(1)} %fusion.20), channel_id=1, source_target_pairs={{0,1},{1,0},{2,3},{3,2},{4,5},{5,4},{6,7},{7,6},{8,9},{9,8},{10,11... | collective-permute-start | bytes 663560 | tf_op jit(solution)/shard_map/rounds/ppermute | solution.py:680
  213.1 7.8 %collective-permute-start.29 = (bf16[48,768]{1,0:T(8,128)(2,1)S(1)}, bf16[48,768]{1,0:T(8,128)(2,1)S(1)}, u32[]{:S(2)}, u32[]{:S(2)}) collective-permute-start(bf16[48,768]{1,0:T(8,128)(2,1)S(1)} %fusion.28), channel_id=1, source_target_pairs={{0,1},{1,0},{2,3},{3,2},{4,5},{5,4},{6,7},{7,6},{8,9},{9,8},{10,11... | collective-permute-start | bytes 221192 | tf_op jit(solution)/shard_map/rounds/ppermute | solution.py:680
  (31 other events, 142.3 us)
where the time goes:
time: 225 us; the launch traced here: 224 us
  Pallas kernels  120 us (53%)
  waiting for transfers between devices  34.3 us (15%)
  starting transfers between devices  32.2 us (14%)
  other arithmetic  19.3 us (9%)
  local copies, waits for them, and re-layouts  16.6 us (7%)
    pallas_call x2, Pallas kernels, attend_back(): pl.pallas_call(functools.partial(attend_back_kernel, seqs=seqs, steps=ste...  40.4 us
    pallas_call x1, Pallas kernels, middle(): pl.pallas_call(functools.partial(middle_kernel, seqs=seqs, chunk=chunk),...  33.8 us
    ppermute x11, waiting for transfers between devices, send(): self.got = lax.ppermute(sent, 'dp', flip('dp', 1 << stage))  19.4 us
    ppermute x11, starting transfers between devices, send(): self.got = lax.ppermute(sent, 'dp', flip('dp', 1 << stage))  15.9 us
    pallas_call x2, Pallas kernels, attend(): pl.pallas_call(functools.partial(attend_kernel, chunk=chunk, seq=seq), gr...  15.5 us
    convert_element_type x21, other arithmetic, joined(): return join([total.astype(BF16) for total in sums], axis)  13.4 us
    ppermute x12, starting transfers between devices, swap_blk(): return lax.ppermute(values, 'blk', flip('blk', 1))  12.3 us
    ppermute x12, waiting for transfers between devices, swap_blk(): return lax.ppermute(values, 'blk', flip('blk', 1))  9.78 us
  transfers between devices with their start and end apart: 32, of which 14 were waited for; matrix products, arithmetic and copies ran while one was open for 12% of the time, Pallas kernels for 33%

commit v1 on v0

--- a/solution.py
+++ b/solution.py
@@ -857,7 +857,7 @@
         hidden_sent = [
             lax.dynamic_slice_in_dim(hidden, (1 - own) * seqs + seq, 1, 0) for seq in each
         ]
-        early = 3 * count // 16
+        early = 2 * count // 16
         upstream_kept = lax.dynamic_slice_in_dim(cotangent, own * seqs, seqs, 0)
         upstream_sent = lax.dynamic_slice_in_dim(cotangent, (1 - own) * seqs, seqs, 0)
         upstream_sent = [upstream_sent[:, :early], upstream_sent[:, early:]]
@@ -959,13 +959,11 @@
     with jax.named_scope("rounds"):
         for shares in (out_shares, in_shares, one_shares):
             shares.send()
+        input_got = swap_blk(input_sent)
         folded = fold_bias(bias_one, length), fold_bias(bias_two, length)
-        *folded, input_sent = receive(
-            [two_shares, one_shares, out_shares, in_shares], *folded, input_sent
-        )
+        folded = receive([two_shares, one_shares, out_shares, in_shares], *folded)
         in_shares.take_over(out_shares)
         in_shares.order = later + ["last"]
-        input_got = swap_blk(input_sent)
         two_shares.send()
         in_shares.send()
 
@@ -993,9 +991,9 @@
 
     with jax.named_scope("rounds"):
         one_shares.send()
-        (flat,) = small_step(flat, [two_shares])
+        flat, input_got = small_step(flat, [two_shares], input_got)
         two_shares.send()
-        flat, input_got = small_step(flat, [two_shares, in_shares], input_got)
+        (flat,) = small_step(flat, [two_shares, in_shares, one_shares])
         chains = [two_shares, one_shares, in_shares]
         while any(shares.order for shares in chains) or small_bits:
             for shares in chains:

time: 225 us -> 224 us (level)
    ppermute x11, waiting for transfers between devices: 19.4 us -> 14.9 us  [send(): self.got = lax.ppermute(sent, 'dp', flip('dp', 1 << stage))]
    ppermute x12, waiting for transfers between devices: 9.78 us -> 14.1 us  [swap_blk(): return lax.ppermute(values, 'blk', flip('blk', 1))]
    unnamed x70 -> x72, local copies, waits for them, and re-layouts: 5.49 us -> 5.3 us
  transfers between devices with their start and end apart: 32 -> 32, of which waited for: 14 -> 13; matrix products, arithmetic and copies ran while one was open for 12% -> 13% of each run, Pallas kernels for 33% -> 33%
where the time goes in v1:
time: 224 us
  Pallas kernels  120 us (54%)
  waiting for transfers between devices  32.7 us (15%)
  starting transfers between devices  31.6 us (14%)
  other arithmetic  20.9 us (9%)
  local copies, waits for them, and re-layouts  16.4 us (7%)
    pallas_call x2, Pallas kernels, attend_back(): pl.pallas_call(functools.partial(attend_back_kernel, seqs=seqs, steps=ste...  40.4 us
    pallas_call x1, Pallas kernels, middle(): pl.pallas_call(functools.partial(middle_kernel, seqs=seqs, chunk=chunk),...  33.8 us
    pallas_call x2, Pallas kernels, attend(): pl.pallas_call(functools.partial(attend_kernel, chunk=chunk, seq=seq), gr...  15.5 us
    ppermute x11, starting transfers between devices, send(): self.got = lax.ppermute(sent, 'dp', flip('dp', 1 << stage))  15 us
    ppermute x11, waiting for transfers between devices, send(): self.got = lax.ppermute(sent, 'dp', flip('dp', 1 << stage))  14.9 us
    ppermute x12, waiting for transfers between devices, swap_blk(): return lax.ppermute(values, 'blk', flip('blk', 1))  14.1 us
    convert_element_type x21, other arithmetic, joined(): return join([total.astype(BF16) for total in sums], axis)  14.1 us
    ppermute x12, starting transfers between devices, swap_blk(): return lax.ppermute(values, 'blk', flip('blk', 1))  12.8 us
  transfers between devices with their start and end apart: 32, of which 13 were waited for; matrix products, arithmetic and copies ran while one was open for 13% of the time, Pallas kernels for 33%

profile of v1, /device:TPU:0, one launch (start us, length us, event | category | flops | bytes accessed | tf_op | source)
XLA Modules:
  0.0 223.6 jit_solution(5478795725653768193)
XLA Ops:
  0.7 1.9 constant_dynamic-slice_fusion.10
  2.6 2.9 %collective-permute-start = (bf16[1,256,768]{2,1,0:T(8,128)(2,1)}, bf16[1,256,768]{2,1,0:T(8,128)(2,1)S(1)}, u32[]{:S(2)}, u32[]{:S(2)}) collective-permute-start(bf16[1,256,768]{2,1,0:T(8,128)(2,1)} %constant_dynamic-slice_fusion.10), channel_id=1, source_target_pairs={{0,1},{1,0},{2,3},{3,2},{4,5},{5,4},{6,7},{7,6},{8,9},{9,8},{10,11... | collective-permute-start | bytes 1179656 | tf_op jit(solution)/shard_map/exchange_in/ppermute | solution.py:680
  9.7 1.9 bias.1.bias_ref
  11.6 2.4 %copy-done.4 = f32[12,128,896]{2,1,0:T(8,128)} copy-done((f32[12,128,896]{2,1,0:T(8,128)}, f32[12,128,896]{2,1,0:T(8,128)S(1)}, u32[]{:S(2)}) %copy-start.4) | copy-done | bytes 5505048
  16.0 1.6 pad_maximum_fusion.w_ref
  17.7 3.3 %project.2 = (bf16[512,768]{1,0:T(8,128)(2,1)S(1)}, bf16[512,768]{1,0:T(8,128)(2,1)S(1)}, bf16[3,512,768]{2,1,0:T(8,128)(2,1)S(1)}) custom-call(s32[2]{0:T(128)S(1)} %pad_add_fusion.scalars, bf16[1,256,768]{2,1,0:T(8,128)(2,1)S(1)} %get-tuple-element.119.kept_ref, bf16[1,256,768]{2,1,0:T(8,128)(2,1)S(1)} %collective-permute-done.got_ref, ...), custom_call_target="tpu_custom_call" | custom-call | flops 1811939328 | bytes 8388608 | tf_op jit(solution)/shard_map/project/pallas_call | solution.py:119
  21.1 2.0 collective-permute-start.2
  23.4 7.7 %attend.2 = (bf16[512,768]{1,0:T(8,128)(2,1)S(1)}, bf16[512,768]{1,0:T(8,128)(2,1)}, bf16[12,512,512]{2,1,0:T(8,128)(2,1)}, f32[512,768]{1,0:T(8,128)}) custom-call(s32[2]{0:T(128)S(1)} %dynamic_slice.214.valid, bf16[3,512,768]{2,1,0:T(8,128)(2,1)S(1)} %get-tuple-element.123.q_ref.k_ref.v_ref.refs_0_.refs_1_.refs_2_, ...), custom_call_target="tpu_custom_call" | custom-call | flops 6442450944 | bytes 12582912 | tf_op jit(solution)/shard_map/attend/pallas_call | solution.py:213
  31.1 2.1 collective-permute-done.1.got_ref
  33.1 3.3 %project.3 = (bf16[512,768]{1,0:T(8,128)(2,1)S(1)}, bf16[512,768]{1,0:T(8,128)(2,1)S(1)}, bf16[3,512,768]{2,1,0:T(8,128)(2,1)S(1)}) custom-call(s32[2]{0:T(128)S(1)} %pad_add_fusion.scalars, bf16[1,256,768]{2,1,0:T(8,128)(2,1)S(1)} %get-tuple-element.127.kept_ref, bf16[1,256,768]{2,1,0:T(8,128)(2,1)S(1)} %collective-permute-done.1.got_ref, ...), custom_call_target="tpu_custom_call" | custom-call | flops 1811939328 | bytes 8388608 | tf_op jit(solution)/shard_map/project/pallas_call | solution.py:119
  36.5 7.8 %attend.3 = (bf16[512,768]{1,0:T(8,128)(2,1)S(1)}, bf16[512,768]{1,0:T(8,128)(2,1)}, bf16[12,512,512]{2,1,0:T(8,128)(2,1)}, f32[512,768]{1,0:T(8,128)}) custom-call(s32[2]{0:T(128)S(1)} %dynamic_slice.214.valid, bf16[3,512,768]{2,1,0:T(8,128)(2,1)S(1)} %get-tuple-element.131.q_ref.k_ref.v_ref.refs_3_.refs_4_.refs_5_, ...), custom_call_target="tpu_custom_call" | custom-call | flops 6442450944 | bytes 12582912 | tf_op jit(solution)/shard_map/attend/pallas_call | solution.py:213
  45.5 3.0 %collective-permute-done.3 = bf16[2,192,768]{2,1,0:T(8,128)(2,1)S(1)} collective-permute-done((bf16[2,192,768]{2,1,0:T(8,128)(2,1)S(1)}, bf16[2,192,768]{2,1,0:T(8,128)(2,1)S(1)}, u32[]{:S(2)}, u32[]{:S(2)}) %collective-permute-start.3) | collective-permute-done | bytes 589856 | tf_op jit(solution)/shard_map/project/ppermute | solution.py:680
  48.6 33.8 %middle.1 = (bf16[1024,3072]{1,0:T(8,128)(2,1)S(1)}, bf16[1024,3072]{1,0:T(8,128)(2,1)S(1)}, bf16[1024,768]{1,0:T(8,128)(2,1)S(1)}, bf16[4,256,768]{2,1,0:T(8,12...) custom-call(s32[2]{0:T(128)S(1)} %pad_add_fusion.scalars, ...), custom_call_target="tpu_custom_call" | custom-call | flops 19327352832 | bytes 20971520 | tf_op jit(solution)/shard_map/middle/pallas_call | solution.py:627
  82.4 7.6 %ffn_weights.2 = (bf16[8,48,3072]{2,1,0:T(8,128)(2,1)}, bf16[8,48,3072]{2,1,0:T(8,128)(2,1)}) custom-call(s32[2]{0:T(128)S(1)} %pad_add_fusion.scalars, bf16[1024,3072]{1,0:T(8,128)(2,1)S(1)} %get-tuple-element.140.act_ref, bf16[1024,768]{1,0:T(8,128)(2,1)S(1)} %bitcast.128), custom_call_target="tpu_custom_call" | custom-call | tf_op jit(solution)/shard_map/ffn_weights/pallas_call | solution.py:524
  90.0 7.5 %ffn_weights.3 = (bf16[8,48,3072]{2,1,0:T(8,128)(2,1)}, bf16[8,48,3072]{2,1,0:T(8,128)(2,1)}) custom-call(s32[2]{0:T(128)S(1)} %pad_add_fusion.scalars, bf16[1024,768]{1,0:T(8,128)(2,1)S(1)} %get-tuple-element.143.ffn_in_ref, bf16[1024,3072]{1,0:T(8,128)(2,1)S(1)} %get-tuple-element.144.pre_ref), custom_call_target="tpu_custom_call" | custom-call | tf_op jit(solution)/shard_map/ffn_weights/pallas_call | solution.py:497
  98.3 2.2 add_convert_fusion.3
  100.5 1.8 collective-permute-start.5
  103.0 1.8 add_convert_fusion.2
  106.0 1.7 add_convert_fusion
  107.7 22.9 %attend_back.2 = (f32[8,128,896]{2,1,0:T(8,128)}, bf16[8,48,1536]{2,1,0:T(8,128)(2,1)}, bf16[8,48,1536]{2,1,0:T(8,128)(2,1)}, bf16[1024,768]{1,0:T(8,128)(2,1)}) custom-call(s32[2]{0:T(128)S(1)} %pad_add_fusion.scalars, bf16[3,512,768]{2,1,0:T(8,128)(2,1)} %copy-done.2, bf16[3,512,768]{2,1,0:T(8,128)(2,1)} %copy-done.2, bf16[3,512,768]{2,1,0:T(8,128)(2,1)} %copy-done.2, ...), custom_call_target="tpu_custom_call" | custom-call | tf_op jit(solution)/shard_map/attend_back/pallas_call | solution.py:465
  137.8 17.6 %attend_back.3 = (f32[4,128,896]{2,1,0:T(8,128)}, bf16[8,48,768]{2,1,0:T(8,128)(2,1)}, bf16[8,48,768]{2,1,0:T(8,128)(2,1)}, bf16[4,256,768]{2,1,0:T(8,128)(2,1)}...) custom-call(s32[2]{0:T(128)S(1)} %pad_add_fusion.scalars, bf16[3,512,768]{2,1,0:T(8,128)(2,1)} %copy-done.2, ...), custom_call_target="tpu_custom_call" | custom-call | tf_op jit(solution)/shard_map/attend_back/pallas_call | solution.py:465
  162.4 3.6 %rounds.2 = f32[8,8,1024]{2,1,0:T(8,128)S(1)} custom-call(f32[8,128,896]{2,1,0:T(8,128)} %get-tuple-element.187.grad_ref), custom_call_target="tpu_custom_call" | custom-call | tf_op jit(solution)/shard_map/rounds/pallas_call | solution.py:80
  166.0 2.6 %rounds.3 = f32[4,8,1024]{2,1,0:T(8,128)S(1)} custom-call(f32[4,128,896]{2,1,0:T(8,128)} %get-tuple-element.188.grad_ref), custom_call_target="tpu_custom_call" | custom-call | tf_op jit(solution)/shard_map/rounds/pallas_call | solution.py:80
  174.7 2.7 %collective-permute-start.23 = (bf16[1,48,3072]{2,1,0:T(8,128)(2,1)S(1)}, bf16[1,48,3072]{2,1,0:T(8,128)(2,1)S(1)}, u32[]{:S(2)}, u32[]{:S(2)}) collective-permute-start(bf16[1,48,3072]{2,1,0:T(8,128)(2,1)S(1)} %pad_maximum_fusion.5), channel_id=1, source_target_pairs={{0,16},{2,18},{4,20},{6,22},{8,24},{10,26},{12,28},{14,30},{16,0},... | collective-permute-start | bytes 884744 | tf_op jit(solution)/shard_map/rounds/ppermute | solution.py:772
  178.1 1.6 collective-permute-start.20
  182.5 4.5 %collective-permute-done.21 = bf16[2,256,768]{2,1,0:T(8,128)(2,1)} collective-permute-done((bf16[2,256,768]{2,1,0:T(8,128)(2,1)}, bf16[2,256,768]{2,1,0:T(8,128)(2,1)}, u32[]{:S(2)}, u32[]{:S(2)}) %collective-permute-start.21) | collective-permute-done | bytes 786464 | tf_op jit(solution)/shard_map/rounds/ppermute | solution.py:680
  190.1 10.5 %collective-permute-done.24 = bf16[1,48,2304]{2,1,0:T(8,128)(2,1)S(1)} collective-permute-done((bf16[1,48,2304]{2,1,0:T(8,128)(2,1)}, bf16[1,48,2304]{2,1,0:T(8,128)(2,1)S(1)}, u32[]{:S(2)}, u32[]{:S(2)}) %collective-permute-start.24) | collective-permute-done | bytes 221216 | tf_op jit(solution)/shard_map/rounds/ppermute | solution.py:772
  200.6 1.6 collective-permute-done.25
  206.1 2.4 %collective-permute-start.26 = (bf16[1,48,768]{2,1,0:T(8,128)(2,1)S(1)}, bf16[1,48,768]{2,1,0:T(8,128)(2,1)S(1)}, u32[]{:S(2)}, u32[]{:S(2)}) collective-permute-start(bf16[1,48,768]{2,1,0:T(8,128)(2,1)S(1)} %fusion.22), channel_id=1, source_target_pairs={{0,16},{2,18},{4,20},{6,22},{8,24},{10,26},{12,28},{14,30},{16,0},... | collective-permute-start | bytes 221192 | tf_op jit(solution)/shard_map/rounds/ppermute | solution.py:772
  209.8 1.7 collective-permute-done.26
  211.4 3.2 %collective-permute-done.27 = bf16[48,2304]{1,0:T(8,128)(2,1)S(1)} collective-permute-done((bf16[48,2304]{1,0:T(8,128)(2,1)S(1)}, bf16[48,2304]{1,0:T(8,128)(2,1)S(1)}, u32[]{:S(2)}, u32[]{:S(2)}) %collective-permute-start.27) | collective-permute-done | bytes 221216 | tf_op jit(solution)/shard_map/rounds/ppermute | solution.py:680
  214.8 1.6 collective-permute-start.31
  (194 shorter events, 49.6 us)
Async XLA Ops:
  2.6 15.1 %collective-permute-start = (bf16[1,256,768]{2,1,0:T(8,128)(2,1)}, bf16[1,256,768]{2,1,0:T(8,128)(2,1)S(1)}, u32[]{:S(2)}, u32[]{:S(2)}) collective-permute-start(bf16[1,256,768]{2,1,0:T(8,128)(2,1)} %constant_dynamic-slice_fusion.10), channel_id=1, source_target_pairs={{0,1},{1,0},{2,3},{3,2},{4,5},{5,4},{6,7},{7,6},{8,9},{9,8},{10,11... | collective-permute-start | bytes 1179656 | tf_op jit(solution)/shard_map/exchange_in/ppermute | solution.py:680
  21.0 12.1 %collective-permute-start.1 = (bf16[1,256,768]{2,1,0:T(8,128)(2,1)S(1)}, bf16[1,256,768]{2,1,0:T(8,128)(2,1)S(1)}, u32[]{:S(2)}, u32[]{:S(2)}) collective-permute-start(bf16[1,256,768]{2,1,0:T(8,128)(2,1)S(1)} %get-tuple-element.116), channel_id=1, source_target_pairs={{0,1},{1,0},{2,3},{3,2},{4,5},{5,4},{6,7},{7,6},{8,9},{9,8},{10,11... | collective-permute-start | bytes 1179656 | tf_op jit(solution)/shard_map/exchange_in/ppermute | solution.py:680
  21.1 27.4 %collective-permute-start.2 = (bf16[2,64,768]{2,1,0:T(8,128)(2,1)S(1)}, bf16[2,64,768]{2,1,0:T(8,128)(2,1)S(1)}, u32[]{:S(2)}, u32[]{:S(2)}) collective-permute-start(bf16[2,64,768]{2,1,0:T(8,128)(2,1)S(1)} %copy-done.17), channel_id=1, source_target_pairs={{0,1},{1,0},{2,3},{3,2},{4,5},{5,4},{6,7},{7,6},{8,9},{9,8},{10,11... | collective-permute-start | bytes 589832 | tf_op jit(solution)/shard_map/project/ppermute | solution.py:680
  33.1 15.4 %collective-permute-start.3 = (bf16[2,192,768]{2,1,0:T(8,128)(2,1)S(1)}, bf16[2,192,768]{2,1,0:T(8,128)(2,1)S(1)}, u32[]{:S(2)}, u32[]{:S(2)}) collective-permute-start(bf16[2,192,768]{2,1,0:T(8,128)(2,1)S(1)} %copy-done.14), channel_id=1, source_target_pairs={{0,1},{1,0},{2,3},{3,2},{4,5},{5,4},{6,7},{7,6},{8,9},{9,8},{10,11... | collective-permute-start | bytes 1769480 | tf_op jit(solution)/shard_map/project/ppermute | solution.py:680
  90.0 7.5 %collective-permute-start.4 = (bf16[8,48,3072]{2,1,0:T(8,128)(2,1)}, bf16[8,48,3072]{2,1,0:T(8,128)(2,1)}, u32[]{:S(2)}, u32[]{:S(2)}) collective-permute-start(bf16[8,48,3072]{2,1,0:T(8,128)(2,1)} %get-tuple-element.142), channel_id=1, source_target_pairs={{0,2},{2,0},{4,6},{6,4},{8,10},{10,8},{12,14},{14,12},{16,18},{18,... | collective-permute-start | bytes 7077896 | tf_op jit(solution)/shard_map/ffn_weights/ppermute | solution.py:755
  97.5 5.5 %collective-permute-start.6 = (bf16[8,48,3072]{2,1,0:T(8,128)(2,1)}, bf16[8,48,3072]{2,1,0:T(8,128)(2,1)}, u32[]{:S(2)}, u32[]{:S(2)}) collective-permute-start(bf16[8,48,3072]{2,1,0:T(8,128)(2,1)} %get-tuple-element.149), channel_id=1, source_target_pairs={{0,2},{2,0},{4,6},{6,4},{8,10},{10,8},{12,14},{14,12},{16,18},{18,... | collective-permute-start | bytes 7077896 | tf_op jit(solution)/shard_map/ffn_weights/ppermute | solution.py:755
  98.0 34.5 %collective-permute-start.8 = (bf16[2,256,768]{2,1,0:T(8,128)(2,1)S(1)}, bf16[2,256,768]{2,1,0:T(8,128)(2,1)S(1)}, u32[]{:S(2)}, u32[]{:S(2)}) collective-permute-start(bf16[2,256,768]{2,1,0:T(8,128)(2,1)S(1)} %copy-done.29), channel_id=1, source_target_pairs={{0,1},{1,0},{2,3},{3,2},{4,5},{5,4},{6,7},{7,6},{8,9},{9,8},{10,11... | collective-permute-start | bytes 2359304 | tf_op jit(solution)/shard_map/output/ppermute | solution.py:680
  98.3 36.0 %collective-permute-start.10 = (bf16[8,48,768]{2,1,0:T(8,128)(2,1)}, bf16[8,48,768]{2,1,0:T(8,128)(2,1)S(1)}, u32[]{:S(2)}, u32[]{:S(2)}) collective-permute-start(bf16[8,48,768]{2,1,0:T(8,128)(2,1)} %get-tuple-element.165), channel_id=1, source_target_pairs={{0,2},{2,0},{4,6},{6,4},{8,10},{10,8},{12,14},{14,12},{16,18},{18,... | collective-permute-start | bytes 1769480 | tf_op jit(solution)/shard_map/attend_back/ppermute | solution.py:755
  100.5 32.1 %collective-permute-start.5 = (bf16[4,48,3072]{2,1,0:T(8,128)(2,1)S(1)}, bf16[4,48,3072]{2,1,0:T(8,128)(2,1)S(1)}, u32[]{:S(2)}, u32[]{:S(2)}) collective-permute-start(bf16[4,48,3072]{2,1,0:T(8,128)(2,1)S(1)} %bitcast.148), channel_id=1, source_target_pairs={{0,4},{2,6},{4,0},{6,2},{8,12},{10,14},{12,8},{14,10},{16,20},{18,... | collective-permute-start | bytes 3538952 | tf_op jit(solution)/shard_map/ffn_weights/ppermute | solution.py:772
  104.8 28.3 %collective-permute-start.7 = (bf16[4,48,3072]{2,1,0:T(8,128)(2,1)S(1)}, bf16[4,48,3072]{2,1,0:T(8,128)(2,1)S(1)}, u32[]{:S(2)}, u32[]{:S(2)}) collective-permute-start(bf16[4,48,3072]{2,1,0:T(8,128)(2,1)S(1)} %bitcast.149), channel_id=1, source_target_pairs={{0,8},{2,10},{4,12},{6,14},{8,0},{10,2},{12,4},{14,6},{16,24},{18,... | collective-permute-start | bytes 3538952 | tf_op jit(solution)/shard_map/ffn_weights/ppermute | solution.py:772
  130.6 3.8 %collective-permute-start.9 = (bf16[8,48,1536]{2,1,0:T(8,128)(2,1)}, bf16[8,48,1536]{2,1,0:T(8,128)(2,1)S(1)}, u32[]{:S(2)}, u32[]{:S(2)}) collective-permute-start(bf16[8,48,1536]{2,1,0:T(8,128)(2,1)} %get-tuple-element.164), channel_id=1, source_target_pairs={{0,2},{2,0},{4,6},{6,4},{8,10},{10,8},{12,14},{14,12},{16,18},{18,... | collective-permute-start | bytes 3538952 | tf_op jit(solution)/shard_map/attend_back/ppermute | solution.py:755
  133.6 22.3 %collective-permute-start.14 = (bf16[4,48,1536]{2,1,0:T(8,128)(2,1)S(1)}, bf16[4,48,1536]{2,1,0:T(8,128)(2,1)S(1)}, u32[]{:S(2)}, u32[]{:S(2)}) collective-permute-start(bf16[4,48,1536]{2,1,0:T(8,128)(2,1)S(1)} %bitcast.158), channel_id=1, source_target_pairs={{0,1},{1,0},{2,3},{3,2},{4,5},{5,4},{6,7},{7,6},{8,9},{9,8},{10,11... | collective-permute-start | bytes 1769480 | tf_op jit(solution)/shard_map/attend_back/ppermute | solution.py:680
  134.9 21.6 %collective-permute-start.12 = (bf16[4,48,2304]{2,1,0:T(8,128)(2,1)S(1)}, bf16[4,48,2304]{2,1,0:T(8,128)(2,1)S(1)}, u32[]{:S(2)}, u32[]{:S(2)}) collective-permute-start(bf16[4,48,2304]{2,1,0:T(8,128)(2,1)S(1)} %pad_maximum_fusion.2), channel_id=1, source_target_pairs={{0,8},{2,10},{4,12},{6,14},{8,0},{10,2},{12,4},{14,6},{16,24},{18,... | collective-permute-start | bytes 2654216 | tf_op jit(solution)/shard_map/attend_back/ppermute | solution.py:772
  136.5 19.4 %collective-permute-start.13 = (bf16[2,48,3072]{2,1,0:T(8,128)(2,1)S(1)}, bf16[2,48,3072]{2,1,0:T(8,128)(2,1)S(1)}, u32[]{:S(2)}, u32[]{:S(2)}) collective-permute-start(bf16[2,48,3072]{2,1,0:T(8,128)(2,1)S(1)} %fusion.5), channel_id=1, source_target_pairs={{0,4},{2,6},{4,0},{6,2},{8,12},{10,14},{12,8},{14,10},{16,20},{18,... | collective-permute-start | bytes 1769480 | tf_op jit(solution)/shard_map/attend_back/ppermute | solution.py:772
  155.3 14.5 %collective-permute-start.11 = (bf16[8,48,768]{2,1,0:T(8,128)(2,1)}, bf16[8,48,768]{2,1,0:T(8,128)(2,1)}, u32[]{:S(2)}, u32[]{:S(2)}) collective-permute-start(bf16[8,48,768]{2,1,0:T(8,128)(2,1)} %get-tuple-element.174), channel_id=1, source_target_pairs={{0,2},{2,0},{4,6},{6,4},{8,10},{10,8},{12,14},{14,12},{16,18},{18,... | collective-permute-start | bytes 1769480 | tf_op jit(solution)/shard_map/attend_back/ppermute | solution.py:755
  157.4 12.5 %collective-permute-start.17 = (bf16[2,48,1536]{2,1,0:T(8,128)(2,1)}, bf16[2,48,1536]{2,1,0:T(8,128)(2,1)S(1)}, u32[]{:S(2)}, u32[]{:S(2)}) collective-permute-start(bf16[2,48,1536]{2,1,0:T(8,128)(2,1)} %get-tuple-element.250), channel_id=1, source_target_pairs={{0,1},{1,0},{2,3},{3,2},{4,5},{5,4},{6,7},{7,6},{8,9},{9,8},{10,11... | collective-permute-start | bytes 884744 | tf_op jit(solution)/shard_map/rounds/ppermute | solution.py:680
  159.6 11.8 %collective-permute-start.15 = (bf16[2,48,2304]{2,1,0:T(8,128)(2,1)}, bf16[2,48,2304]{2,1,0:T(8,128)(2,1)S(1)}, u32[]{:S(2)}, u32[]{:S(2)}) collective-permute-start(bf16[2,48,2304]{2,1,0:T(8,128)(2,1)} %get-tuple-element.231), channel_id=1, source_target_pairs={{0,4},{2,6},{4,0},{6,2},{8,12},{10,14},{12,8},{14,10},{16,20},{18,... | collective-permute-start | bytes 1327112 | tf_op jit(solution)/shard_map/rounds/ppermute | solution.py:772
  161.5 8.3 %collective-permute-start.16 = (bf16[2,48,1536]{2,1,0:T(8,128)(2,1)}, bf16[2,48,1536]{2,1,0:T(8,128)(2,1)S(1)}, u32[]{:S(2)}, u32[]{:S(2)}) collective-permute-start(bf16[2,48,1536]{2,1,0:T(8,128)(2,1)} %get-tuple-element.236), channel_id=1, source_target_pairs={{0,8},{2,10},{4,12},{6,14},{8,0},{10,2},{12,4},{14,6},{16,24},{18,... | collective-permute-start | bytes 884744 | tf_op jit(solution)/shard_map/rounds/ppermute | solution.py:772
  168.6 18.4 %collective-permute-start.21 = (bf16[2,256,768]{2,1,0:T(8,128)(2,1)}, bf16[2,256,768]{2,1,0:T(8,128)(2,1)}, u32[]{:S(2)}, u32[]{:S(2)}) collective-permute-start(bf16[2,256,768]{2,1,0:T(8,128)(2,1)} %get-tuple-element.194), channel_id=1, source_target_pairs={{0,1},{1,0},{2,3},{3,2},{4,5},{5,4},{6,7},{7,6},{8,9},{9,8},{10,11... | collective-permute-start | bytes 2359304 | tf_op jit(solution)/shard_map/rounds/ppermute | solution.py:680
  171.7 6.3 %collective-permute-start.19 = (f32[16,128]{1,0:T(8,128)S(1)}, f32[16,128]{1,0:T(8,128)S(1)}, u32[]{:S(2)}, u32[]{:S(2)}) collective-permute-start(f32[16,128]{1,0:T(8,128)S(1)} %fusion.32), channel_id=1, source_target_pairs={{0,2},{2,0},{4,6},{6,4},{8,10},{10,8},{12,14},{14,12},{16,18},{18,... | collective-permute-start | bytes 24584 | tf_op jit(solution)/shard_map/small/ppermute | solution.py:980
  172.9 9.6 %collective-permute-start.18 = (bf16[4,48,768]{2,1,0:T(8,128)(2,1)S(1)}, bf16[4,48,768]{2,1,0:T(8,128)(2,1)S(1)}, u32[]{:S(2)}, u32[]{:S(2)}) collective-permute-start(bf16[4,48,768]{2,1,0:T(8,128)(2,1)S(1)} %bitcast.159), channel_id=1, source_target_pairs={{0,4},{2,6},{4,0},{6,2},{8,12},{10,14},{12,8},{14,10},{16,20},{18,... | collective-permute-start | bytes 884744 | tf_op jit(solution)/shard_map/rounds/ppermute | solution.py:772
  174.7 26.0 %collective-permute-start.23 = (bf16[1,48,3072]{2,1,0:T(8,128)(2,1)S(1)}, bf16[1,48,3072]{2,1,0:T(8,128)(2,1)S(1)}, u32[]{:S(2)}, u32[]{:S(2)}) collective-permute-start(bf16[1,48,3072]{2,1,0:T(8,128)(2,1)S(1)} %pad_maximum_fusion.5), channel_id=1, source_target_pairs={{0,16},{2,18},{4,20},{6,22},{8,24},{10,26},{12,28},{14,30},{16,0},... | collective-permute-start | bytes 884744 | tf_op jit(solution)/shard_map/rounds/ppermute | solution.py:772
  178.1 4.4 %collective-permute-start.20 = (f32[16,128]{1,0:T(8,128)S(1)}, f32[16,128]{1,0:T(8,128)S(1)}, u32[]{:S(2)}, u32[]{:S(2)}) collective-permute-start(f32[16,128]{1,0:T(8,128)S(1)} %fusion.42), channel_id=1, source_target_pairs={{0,4},{2,6},{4,0},{6,2},{8,12},{10,14},{12,8},{14,10},{16,20},{18,... | collective-permute-start | bytes 24584 | tf_op jit(solution)/shard_map/rounds/ppermute | solution.py:988
  180.7 20.0 %collective-permute-start.24 = (bf16[1,48,2304]{2,1,0:T(8,128)(2,1)}, bf16[1,48,2304]{2,1,0:T(8,128)(2,1)S(1)}, u32[]{:S(2)}, u32[]{:S(2)}) collective-permute-start(bf16[1,48,2304]{2,1,0:T(8,128)(2,1)} %fusion.12), channel_id=1, source_target_pairs={{0,16},{2,18},{4,20},{6,22},{8,24},{10,26},{12,28},{14,30},{16,0},... | collective-permute-start | bytes 663560 | tf_op jit(solution)/shard_map/rounds/ppermute | solution.py:772
  187.1 15.1 %collective-permute-start.22 = (bf16[2,48,768]{2,1,0:T(8,128)(2,1)S(1)}, bf16[2,48,768]{2,1,0:T(8,128)(2,1)S(1)}, u32[]{:S(2)}, u32[]{:S(2)}) collective-permute-start(bf16[2,48,768]{2,1,0:T(8,128)(2,1)S(1)} %get-tuple-element.248), channel_id=1, source_target_pairs={{0,8},{2,10},{4,12},{6,14},{8,0},{10,2},{12,4},{14,6},{16,24},{18,... | collective-permute-start | bytes 442376 | tf_op jit(solution)/shard_map/rounds/ppermute | solution.py:772
  188.3 13.9 %collective-permute-start.25 = (f32[16,128]{1,0:T(8,128)S(1)}, f32[16,128]{1,0:T(8,128)S(1)}, u32[]{:S(2)}, u32[]{:S(2)}) collective-permute-start(f32[16,128]{1,0:T(8,128)S(1)} %add.312), channel_id=1, source_target_pairs={{0,8},{2,10},{4,12},{6,14},{8,0},{10,2},{12,4},{14,6},{16,24},{18,... | collective-permute-start | bytes 24584 | tf_op jit(solution)/shard_map/rounds/ppermute | solution.py:988
  202.2 7.5 %collective-permute-start.29 = (f32[16,128]{1,0:T(8,128)S(1)}, f32[16,128]{1,0:T(8,128)S(1)}, u32[]{:S(2)}, u32[]{:S(2)}) collective-permute-start(f32[16,128]{1,0:T(8,128)S(1)} %add.320), channel_id=1, source_target_pairs={{0,16},{2,18},{4,20},{6,22},{8,24},{10,26},{12,28},{14,30},{16,0},... | collective-permute-start | bytes 24584 | tf_op jit(solution)/shard_map/rounds/ppermute | solution.py:988
  202.9 11.7 %collective-permute-start.28 = (bf16[48,3072]{1,0:T(8,128)(2,1)S(1)}, bf16[48,3072]{1,0:T(8,128)(2,1)S(1)}, u32[]{:S(2)}, u32[]{:S(2)}) collective-permute-start(bf16[48,3072]{1,0:T(8,128)(2,1)S(1)} %get-tuple-element.227), channel_id=1, source_target_pairs={{0,1},{1,0},{2,3},{3,2},{4,5},{5,4},{6,7},{7,6},{8,9},{9,8},{10,11... | collective-permute-start | bytes 884744 | tf_op jit(solution)/shard_map/rounds/ppermute | solution.py:680
  205.1 9.5 %collective-permute-start.27 = (bf16[48,2304]{1,0:T(8,128)(2,1)S(1)}, bf16[48,2304]{1,0:T(8,128)(2,1)S(1)}, u32[]{:S(2)}, u32[]{:S(2)}) collective-permute-start(bf16[48,2304]{1,0:T(8,128)(2,1)S(1)} %fusion.20), channel_id=1, source_target_pairs={{0,1},{1,0},{2,3},{3,2},{4,5},{5,4},{6,7},{7,6},{8,9},{9,8},{10,11... | collective-permute-start | bytes 663560 | tf_op jit(solution)/shard_map/rounds/ppermute | solution.py:680
  206.1 5.3 %collective-permute-start.26 = (bf16[1,48,768]{2,1,0:T(8,128)(2,1)S(1)}, bf16[1,48,768]{2,1,0:T(8,128)(2,1)S(1)}, u32[]{:S(2)}, u32[]{:S(2)}) collective-permute-start(bf16[1,48,768]{2,1,0:T(8,128)(2,1)S(1)} %fusion.22), channel_id=1, source_target_pairs={{0,16},{2,18},{4,20},{6,22},{8,24},{10,26},{12,28},{14,30},{16,0},... | collective-permute-start | bytes 221192 | tf_op jit(solution)/shard_map/rounds/ppermute | solution.py:772
  214.8 4.7 %collective-permute-start.31 = (f32[16,128]{1,0:T(8,128)S(1)}, f32[16,128]{1,0:T(8,128)S(1)}, u32[]{:S(2)}, u32[]{:S(2)}) collective-permute-start(f32[16,128]{1,0:T(8,128)S(1)} %add.322), channel_id=1, source_target_pairs={{0,1},{1,0},{2,3},{3,2},{4,5},{5,4},{6,7},{7,6},{8,9},{9,8},{10,11... | collective-permute-start | bytes 24584 | tf_op jit(solution)/shard_map/rounds/ppermute | solution.py:680
  216.4 4.4 %collective-permute-start.30 = (bf16[48,768]{1,0:T(8,128)(2,1)S(1)}, bf16[48,768]{1,0:T(8,128)(2,1)S(1)}, u32[]{:S(2)}, u32[]{:S(2)}) collective-permute-start(bf16[48,768]{1,0:T(8,128)(2,1)S(1)} %fusion.28), channel_id=1, source_target_pairs={{0,1},{1,0},{2,3},{3,2},{4,5},{5,4},{6,7},{7,6},{8,9},{9,8},{10,11... | collective-permute-start | bytes 221192 | tf_op jit(solution)/shard_map/rounds/ppermute | solution.py:680
  (32 other events, 139.3 us)

commit v2 on v1

--- a/solution.py
+++ b/solution.py
@@ -1021,8 +1021,8 @@
         flat = flat.reshape(-1)
         share = width // size
         at = lax.axis_index("dp") * share
-        gain_attn = lax.dynamic_slice_in_dim(flat[:width], at, share)
-        gain_ffn = lax.dynamic_slice_in_dim(flat[width : 2 * width], at, share)
+        gains = flat[: 2 * width].reshape(2, width)
+        gain_attn, gain_ffn = lax.dynamic_slice_in_dim(gains, at, share, 1)
         table = flat[2 * width : 2 * width + buckets_used * heads].reshape(buckets_used, heads)
 
     return (

time: 224 us -> 224 us (level)
  transfers between devices with their start and end apart: 32 -> 32, of which waited for: 13 -> 13; matrix products, arithmetic and copies ran while one was open for 13% -> 13% of each run, Pallas kernels for 33% -> 34%
where the time goes in v2:
time: 224 us; the launch traced here: 223 us
  Pallas kernels  120 us (54%)
  waiting for transfers between devices  32.7 us (15%)
  starting transfers between devices  31.6 us (14%)
  other arithmetic  20.9 us (9%)
  local copies, waits for them, and re-layouts  15.8 us (7%)
    pallas_call x2, Pallas kernels, attend_back(): pl.pallas_call(functools.partial(attend_back_kernel, seqs=seqs, steps=ste...  40.4 us
    pallas_call x1, Pallas kernels, middle(): pl.pallas_call(functools.partial(middle_kernel, seqs=seqs, chunk=chunk),...  33.8 us
    pallas_call x2, Pallas kernels, attend(): pl.pallas_call(functools.partial(attend_kernel, chunk=chunk, seq=seq), gr...  15.5 us
    ppermute x11, starting transfers between devices, send(): self.got = lax.ppermute(sent, 'dp', flip('dp', 1 << stage))  15 us
    ppermute x11, waiting for transfers between devices, send(): self.got = lax.ppermute(sent, 'dp', flip('dp', 1 << stage))  14.9 us
    ppermute x12, waiting for transfers between devices, swap_blk(): return lax.ppermute(values, 'blk', flip('blk', 1))  14.1 us
    convert_element_type x21, other arithmetic, joined(): return join([total.astype(BF16) for total in sums], axis)  14.1 us
    ppermute x12, starting transfers between devices, swap_blk(): return lax.ppermute(values, 'blk', flip('blk', 1))  12.8 us
  transfers between devices with their start and end apart: 32, of which 13 were waited for; matrix products, arithmetic and copies ran while one was open for 13% of the time, Pallas kernels for 34%

profile of v2, /device:TPU:0, one launch (start us, length us, event | category | flops | bytes accessed | tf_op | source)
XLA Modules:
  0.0 223.1 jit_solution(10430935133872995330)
XLA Ops:
  0.7 1.9 constant_dynamic-slice_fusion.11
  2.6 2.9 %collective-permute-start = (bf16[1,256,768]{2,1,0:T(8,128)(2,1)}, bf16[1,256,768]{2,1,0:T(8,128)(2,1)S(1)}, u32[]{:S(2)}, u32[]{:S(2)}) collective-permute-start(bf16[1,256,768]{2,1,0:T(8,128)(2,1)} %constant_dynamic-slice_fusion.11), channel_id=1, source_target_pairs={{0,1},{1,0},{2,3},{3,2},{4,5},{5,4},{6,7},{7,6},{8,9},{9,8},{10,11... | collective-permute-start | bytes 1179656 | tf_op jit(solution)/shard_map/exchange_in/ppermute | solution.py:680
  9.7 1.9 bias.1.bias_ref
  11.6 2.4 %copy-done.4 = f32[12,128,896]{2,1,0:T(8,128)} copy-done((f32[12,128,896]{2,1,0:T(8,128)}, f32[12,128,896]{2,1,0:T(8,128)S(1)}, u32[]{:S(2)}) %copy-start.4) | copy-done | bytes 5505048
  16.0 1.6 pad_maximum_fusion.w_ref
  17.7 3.3 %project.2 = (bf16[512,768]{1,0:T(8,128)(2,1)S(1)}, bf16[512,768]{1,0:T(8,128)(2,1)S(1)}, bf16[3,512,768]{2,1,0:T(8,128)(2,1)S(1)}) custom-call(s32[2]{0:T(128)S(1)} %pad_add_fusion.scalars, bf16[1,256,768]{2,1,0:T(8,128)(2,1)S(1)} %get-tuple-element.119.kept_ref, bf16[1,256,768]{2,1,0:T(8,128)(2,1)S(1)} %collective-permute-done.got_ref, ...), custom_call_target="tpu_custom_call" | custom-call | flops 1811939328 | bytes 8388608 | tf_op jit(solution)/shard_map/project/pallas_call | solution.py:119
  21.1 2.0 collective-permute-start.2
  23.4 7.7 %attend.2 = (bf16[512,768]{1,0:T(8,128)(2,1)S(1)}, bf16[512,768]{1,0:T(8,128)(2,1)}, bf16[12,512,512]{2,1,0:T(8,128)(2,1)}, f32[512,768]{1,0:T(8,128)}) custom-call(s32[2]{0:T(128)S(1)} %dynamic_slice.211.valid, bf16[3,512,768]{2,1,0:T(8,128)(2,1)S(1)} %get-tuple-element.123.q_ref.k_ref.v_ref.refs_0_.refs_1_.refs_2_, ...), custom_call_target="tpu_custom_call" | custom-call | flops 6442450944 | bytes 12582912 | tf_op jit(solution)/shard_map/attend/pallas_call | solution.py:213
  31.1 2.1 collective-permute-done.1.got_ref
  33.1 3.3 %project.3 = (bf16[512,768]{1,0:T(8,128)(2,1)S(1)}, bf16[512,768]{1,0:T(8,128)(2,1)S(1)}, bf16[3,512,768]{2,1,0:T(8,128)(2,1)S(1)}) custom-call(s32[2]{0:T(128)S(1)} %pad_add_fusion.scalars, bf16[1,256,768]{2,1,0:T(8,128)(2,1)S(1)} %get-tuple-element.127.kept_ref, bf16[1,256,768]{2,1,0:T(8,128)(2,1)S(1)} %collective-permute-done.1.got_ref, ...), custom_call_target="tpu_custom_call" | custom-call | flops 1811939328 | bytes 8388608 | tf_op jit(solution)/shard_map/project/pallas_call | solution.py:119
  36.5 7.8 %attend.3 = (bf16[512,768]{1,0:T(8,128)(2,1)S(1)}, bf16[512,768]{1,0:T(8,128)(2,1)}, bf16[12,512,512]{2,1,0:T(8,128)(2,1)}, f32[512,768]{1,0:T(8,128)}) custom-call(s32[2]{0:T(128)S(1)} %dynamic_slice.211.valid, bf16[3,512,768]{2,1,0:T(8,128)(2,1)S(1)} %get-tuple-element.131.q_ref.k_ref.v_ref.refs_3_.refs_4_.refs_5_, ...), custom_call_target="tpu_custom_call" | custom-call | flops 6442450944 | bytes 12582912 | tf_op jit(solution)/shard_map/attend/pallas_call | solution.py:213
  45.5 3.0 %collective-permute-done.3 = bf16[2,192,768]{2,1,0:T(8,128)(2,1)S(1)} collective-permute-done((bf16[2,192,768]{2,1,0:T(8,128)(2,1)S(1)}, bf16[2,192,768]{2,1,0:T(8,128)(2,1)S(1)}, u32[]{:S(2)}, u32[]{:S(2)}) %collective-permute-start.3) | collective-permute-done | bytes 589856 | tf_op jit(solution)/shard_map/project/ppermute | solution.py:680
  48.6 33.8 %middle.1 = (bf16[1024,3072]{1,0:T(8,128)(2,1)S(1)}, bf16[1024,3072]{1,0:T(8,128)(2,1)S(1)}, bf16[1024,768]{1,0:T(8,128)(2,1)S(1)}, bf16[4,256,768]{2,1,0:T(8,12...) custom-call(s32[2]{0:T(128)S(1)} %pad_add_fusion.scalars, ...), custom_call_target="tpu_custom_call" | custom-call | flops 19327352832 | bytes 20971520 | tf_op jit(solution)/shard_map/middle/pallas_call | solution.py:627
  82.4 7.6 %ffn_weights.2 = (bf16[8,48,3072]{2,1,0:T(8,128)(2,1)}, bf16[8,48,3072]{2,1,0:T(8,128)(2,1)}) custom-call(s32[2]{0:T(128)S(1)} %pad_add_fusion.scalars, bf16[1024,3072]{1,0:T(8,128)(2,1)S(1)} %get-tuple-element.140.act_ref, bf16[1024,768]{1,0:T(8,128)(2,1)S(1)} %bitcast.129), custom_call_target="tpu_custom_call" | custom-call | tf_op jit(solution)/shard_map/ffn_weights/pallas_call | solution.py:524
  90.0 7.5 %ffn_weights.3 = (bf16[8,48,3072]{2,1,0:T(8,128)(2,1)}, bf16[8,48,3072]{2,1,0:T(8,128)(2,1)}) custom-call(s32[2]{0:T(128)S(1)} %pad_add_fusion.scalars, bf16[1024,768]{1,0:T(8,128)(2,1)S(1)} %get-tuple-element.143.ffn_in_ref, bf16[1024,3072]{1,0:T(8,128)(2,1)S(1)} %get-tuple-element.144.pre_ref), custom_call_target="tpu_custom_call" | custom-call | tf_op jit(solution)/shard_map/ffn_weights/pallas_call | solution.py:497
  98.3 2.2 add_convert_fusion.3
  100.5 1.8 collective-permute-start.5
  103.0 1.8 add_convert_fusion.2
  106.0 1.7 add_convert_fusion
  107.7 22.9 %attend_back.2 = (f32[8,128,896]{2,1,0:T(8,128)}, bf16[8,48,1536]{2,1,0:T(8,128)(2,1)}, bf16[8,48,1536]{2,1,0:T(8,128)(2,1)}, bf16[1024,768]{1,0:T(8,128)(2,1)}) custom-call(s32[2]{0:T(128)S(1)} %pad_add_fusion.scalars, bf16[3,512,768]{2,1,0:T(8,128)(2,1)} %copy-done.2, bf16[3,512,768]{2,1,0:T(8,128)(2,1)} %copy-done.2, bf16[3,512,768]{2,1,0:T(8,128)(2,1)} %copy-done.2, ...), custom_call_target="tpu_custom_call" | custom-call | tf_op jit(solution)/shard_map/attend_back/pallas_call | solution.py:465
  137.8 17.6 %attend_back.3 = (f32[4,128,896]{2,1,0:T(8,128)}, bf16[8,48,768]{2,1,0:T(8,128)(2,1)}, bf16[8,48,768]{2,1,0:T(8,128)(2,1)}, bf16[4,256,768]{2,1,0:T(8,128)(2,1)}...) custom-call(s32[2]{0:T(128)S(1)} %pad_add_fusion.scalars, bf16[3,512,768]{2,1,0:T(8,128)(2,1)} %copy-done.2, ...), custom_call_target="tpu_custom_call" | custom-call | tf_op jit(solution)/shard_map/attend_back/pallas_call | solution.py:465
  162.4 3.6 %rounds.2 = f32[8,8,1024]{2,1,0:T(8,128)S(1)} custom-call(f32[8,128,896]{2,1,0:T(8,128)} %get-tuple-element.187.grad_ref), custom_call_target="tpu_custom_call" | custom-call | tf_op jit(solution)/shard_map/rounds/pallas_call | solution.py:80
  166.0 2.6 %rounds.3 = f32[4,8,1024]{2,1,0:T(8,128)S(1)} custom-call(f32[4,128,896]{2,1,0:T(8,128)} %get-tuple-element.188.grad_ref), custom_call_target="tpu_custom_call" | custom-call | tf_op jit(solution)/shard_map/rounds/pallas_call | solution.py:80
  174.7 2.7 %collective-permute-start.23 = (bf16[1,48,3072]{2,1,0:T(8,128)(2,1)S(1)}, bf16[1,48,3072]{2,1,0:T(8,128)(2,1)S(1)}, u32[]{:S(2)}, u32[]{:S(2)}) collective-permute-start(bf16[1,48,3072]{2,1,0:T(8,128)(2,1)S(1)} %pad_maximum_fusion.5), channel_id=1, source_target_pairs={{0,16},{2,18},{4,20},{6,22},{8,24},{10,26},{12,28},{14,30},{16,0},... | collective-permute-start | bytes 884744 | tf_op jit(solution)/shard_map/rounds/ppermute | solution.py:772
  178.1 1.6 collective-permute-start.20
  182.5 4.5 %collective-permute-done.21 = bf16[2,256,768]{2,1,0:T(8,128)(2,1)} collective-permute-done((bf16[2,256,768]{2,1,0:T(8,128)(2,1)}, bf16[2,256,768]{2,1,0:T(8,128)(2,1)}, u32[]{:S(2)}, u32[]{:S(2)}) %collective-permute-start.21) | collective-permute-done | bytes 786464 | tf_op jit(solution)/shard_map/rounds/ppermute | solution.py:680
  190.1 10.5 %collective-permute-done.24 = bf16[1,48,2304]{2,1,0:T(8,128)(2,1)S(1)} collective-permute-done((bf16[1,48,2304]{2,1,0:T(8,128)(2,1)}, bf16[1,48,2304]{2,1,0:T(8,128)(2,1)S(1)}, u32[]{:S(2)}, u32[]{:S(2)}) %collective-permute-start.24) | collective-permute-done | bytes 221216 | tf_op jit(solution)/shard_map/rounds/ppermute | solution.py:772
  200.6 1.6 collective-permute-done.25
  206.1 2.4 %collective-permute-start.26 = (bf16[1,48,768]{2,1,0:T(8,128)(2,1)S(1)}, bf16[1,48,768]{2,1,0:T(8,128)(2,1)S(1)}, u32[]{:S(2)}, u32[]{:S(2)}) collective-permute-start(bf16[1,48,768]{2,1,0:T(8,128)(2,1)S(1)} %fusion.22), channel_id=1, source_target_pairs={{0,16},{2,18},{4,20},{6,22},{8,24},{10,26},{12,28},{14,30},{16,0},... | collective-permute-start | bytes 221192 | tf_op jit(solution)/shard_map/rounds/ppermute | solution.py:772
  209.8 1.7 collective-permute-done.26
  211.4 3.2 %collective-permute-done.27 = bf16[48,2304]{1,0:T(8,128)(2,1)S(1)} collective-permute-done((bf16[48,2304]{1,0:T(8,128)(2,1)S(1)}, bf16[48,2304]{1,0:T(8,128)(2,1)S(1)}, u32[]{:S(2)}, u32[]{:S(2)}) %collective-permute-start.27) | collective-permute-done | bytes 221216 | tf_op jit(solution)/shard_map/rounds/ppermute | solution.py:680
  214.8 1.6 collective-permute-start.31
  (194 shorter events, 49.0 us)
Async XLA Ops:
  2.6 15.1 %collective-permute-start = (bf16[1,256,768]{2,1,0:T(8,128)(2,1)}, bf16[1,256,768]{2,1,0:T(8,128)(2,1)S(1)}, u32[]{:S(2)}, u32[]{:S(2)}) collective-permute-start(bf16[1,256,768]{2,1,0:T(8,128)(2,1)} %constant_dynamic-slice_fusion.11), channel_id=1, source_target_pairs={{0,1},{1,0},{2,3},{3,2},{4,5},{5,4},{6,7},{7,6},{8,9},{9,8},{10,11... | collective-permute-start | bytes 1179656 | tf_op jit(solution)/shard_map/exchange_in/ppermute | solution.py:680
  21.0 12.1 %collective-permute-start.1 = (bf16[1,256,768]{2,1,0:T(8,128)(2,1)S(1)}, bf16[1,256,768]{2,1,0:T(8,128)(2,1)S(1)}, u32[]{:S(2)}, u32[]{:S(2)}) collective-permute-start(bf16[1,256,768]{2,1,0:T(8,128)(2,1)S(1)} %get-tuple-element.116), channel_id=1, source_target_pairs={{0,1},{1,0},{2,3},{3,2},{4,5},{5,4},{6,7},{7,6},{8,9},{9,8},{10,11... | collective-permute-start | bytes 1179656 | tf_op jit(solution)/shard_map/exchange_in/ppermute | solution.py:680
  21.1 27.4 %collective-permute-start.2 = (bf16[2,64,768]{2,1,0:T(8,128)(2,1)S(1)}, bf16[2,64,768]{2,1,0:T(8,128)(2,1)S(1)}, u32[]{:S(2)}, u32[]{:S(2)}) collective-permute-start(bf16[2,64,768]{2,1,0:T(8,128)(2,1)S(1)} %copy-done.17), channel_id=1, source_target_pairs={{0,1},{1,0},{2,3},{3,2},{4,5},{5,4},{6,7},{7,6},{8,9},{9,8},{10,11... | collective-permute-start | bytes 589832 | tf_op jit(solution)/shard_map/project/ppermute | solution.py:680
  33.1 15.4 %collective-permute-start.3 = (bf16[2,192,768]{2,1,0:T(8,128)(2,1)S(1)}, bf16[2,192,768]{2,1,0:T(8,128)(2,1)S(1)}, u32[]{:S(2)}, u32[]{:S(2)}) collective-permute-start(bf16[2,192,768]{2,1,0:T(8,128)(2,1)S(1)} %copy-done.14), channel_id=1, source_target_pairs={{0,1},{1,0},{2,3},{3,2},{4,5},{5,4},{6,7},{7,6},{8,9},{9,8},{10,11... | collective-permute-start | bytes 1769480 | tf_op jit(solution)/shard_map/project/ppermute | solution.py:680
  90.0 7.5 %collective-permute-start.4 = (bf16[8,48,3072]{2,1,0:T(8,128)(2,1)}, bf16[8,48,3072]{2,1,0:T(8,128)(2,1)}, u32[]{:S(2)}, u32[]{:S(2)}) collective-permute-start(bf16[8,48,3072]{2,1,0:T(8,128)(2,1)} %get-tuple-element.142), channel_id=1, source_target_pairs={{0,2},{2,0},{4,6},{6,4},{8,10},{10,8},{12,14},{14,12},{16,18},{18,... | collective-permute-start | bytes 7077896 | tf_op jit(solution)/shard_map/ffn_weights/ppermute | solution.py:755
  97.5 5.5 %collective-permute-start.6 = (bf16[8,48,3072]{2,1,0:T(8,128)(2,1)}, bf16[8,48,3072]{2,1,0:T(8,128)(2,1)}, u32[]{:S(2)}, u32[]{:S(2)}) collective-permute-start(bf16[8,48,3072]{2,1,0:T(8,128)(2,1)} %get-tuple-element.149), channel_id=1, source_target_pairs={{0,2},{2,0},{4,6},{6,4},{8,10},{10,8},{12,14},{14,12},{16,18},{18,... | collective-permute-start | bytes 7077896 | tf_op jit(solution)/shard_map/ffn_weights/ppermute | solution.py:755
  98.0 34.5 %collective-permute-start.8 = (bf16[2,256,768]{2,1,0:T(8,128)(2,1)S(1)}, bf16[2,256,768]{2,1,0:T(8,128)(2,1)S(1)}, u32[]{:S(2)}, u32[]{:S(2)}) collective-permute-start(bf16[2,256,768]{2,1,0:T(8,128)(2,1)S(1)} %copy-done.29), channel_id=1, source_target_pairs={{0,1},{1,0},{2,3},{3,2},{4,5},{5,4},{6,7},{7,6},{8,9},{9,8},{10,11... | collective-permute-start | bytes 2359304 | tf_op jit(solution)/shard_map/output/ppermute | solution.py:680
  98.3 36.0 %collective-permute-start.10 = (bf16[8,48,768]{2,1,0:T(8,128)(2,1)}, bf16[8,48,768]{2,1,0:T(8,128)(2,1)S(1)}, u32[]{:S(2)}, u32[]{:S(2)}) collective-permute-start(bf16[8,48,768]{2,1,0:T(8,128)(2,1)} %get-tuple-element.165), channel_id=1, source_target_pairs={{0,2},{2,0},{4,6},{6,4},{8,10},{10,8},{12,14},{14,12},{16,18},{18,... | collective-permute-start | bytes 1769480 | tf_op jit(solution)/shard_map/attend_back/ppermute | solution.py:755
  100.5 32.1 %collective-permute-start.5 = (bf16[4,48,3072]{2,1,0:T(8,128)(2,1)S(1)}, bf16[4,48,3072]{2,1,0:T(8,128)(2,1)S(1)}, u32[]{:S(2)}, u32[]{:S(2)}) collective-permute-start(bf16[4,48,3072]{2,1,0:T(8,128)(2,1)S(1)} %bitcast.149), channel_id=1, source_target_pairs={{0,4},{2,6},{4,0},{6,2},{8,12},{10,14},{12,8},{14,10},{16,20},{18,... | collective-permute-start | bytes 3538952 | tf_op jit(solution)/shard_map/ffn_weights/ppermute | solution.py:772
  104.8 28.3 %collective-permute-start.7 = (bf16[4,48,3072]{2,1,0:T(8,128)(2,1)S(1)}, bf16[4,48,3072]{2,1,0:T(8,128)(2,1)S(1)}, u32[]{:S(2)}, u32[]{:S(2)}) collective-permute-start(bf16[4,48,3072]{2,1,0:T(8,128)(2,1)S(1)} %bitcast.150), channel_id=1, source_target_pairs={{0,8},{2,10},{4,12},{6,14},{8,0},{10,2},{12,4},{14,6},{16,24},{18,... | collective-permute-start | bytes 3538952 | tf_op jit(solution)/shard_map/ffn_weights/ppermute | solution.py:772
  130.6 3.8 %collective-permute-start.9 = (bf16[8,48,1536]{2,1,0:T(8,128)(2,1)}, bf16[8,48,1536]{2,1,0:T(8,128)(2,1)S(1)}, u32[]{:S(2)}, u32[]{:S(2)}) collective-permute-start(bf16[8,48,1536]{2,1,0:T(8,128)(2,1)} %get-tuple-element.164), channel_id=1, source_target_pairs={{0,2},{2,0},{4,6},{6,4},{8,10},{10,8},{12,14},{14,12},{16,18},{18,... | collective-permute-start | bytes 3538952 | tf_op jit(solution)/shard_map/attend_back/ppermute | solution.py:755
  133.6 22.3 %collective-permute-start.14 = (bf16[4,48,1536]{2,1,0:T(8,128)(2,1)S(1)}, bf16[4,48,1536]{2,1,0:T(8,128)(2,1)S(1)}, u32[]{:S(2)}, u32[]{:S(2)}) collective-permute-start(bf16[4,48,1536]{2,1,0:T(8,128)(2,1)S(1)} %bitcast.159), channel_id=1, source_target_pairs={{0,1},{1,0},{2,3},{3,2},{4,5},{5,4},{6,7},{7,6},{8,9},{9,8},{10,11... | collective-permute-start | bytes 1769480 | tf_op jit(solution)/shard_map/attend_back/ppermute | solution.py:680
  134.9 21.6 %collective-permute-start.12 = (bf16[4,48,2304]{2,1,0:T(8,128)(2,1)S(1)}, bf16[4,48,2304]{2,1,0:T(8,128)(2,1)S(1)}, u32[]{:S(2)}, u32[]{:S(2)}) collective-permute-start(bf16[4,48,2304]{2,1,0:T(8,128)(2,1)S(1)} %pad_maximum_fusion.2), channel_id=1, source_target_pairs={{0,8},{2,10},{4,12},{6,14},{8,0},{10,2},{12,4},{14,6},{16,24},{18,... | collective-permute-start | bytes 2654216 | tf_op jit(solution)/shard_map/attend_back/ppermute | solution.py:772
  136.5 19.4 %collective-permute-start.13 = (bf16[2,48,3072]{2,1,0:T(8,128)(2,1)S(1)}, bf16[2,48,3072]{2,1,0:T(8,128)(2,1)S(1)}, u32[]{:S(2)}, u32[]{:S(2)}) collective-permute-start(bf16[2,48,3072]{2,1,0:T(8,128)(2,1)S(1)} %fusion.5), channel_id=1, source_target_pairs={{0,4},{2,6},{4,0},{6,2},{8,12},{10,14},{12,8},{14,10},{16,20},{18,... | collective-permute-start | bytes 1769480 | tf_op jit(solution)/shard_map/attend_back/ppermute | solution.py:772
  155.3 14.5 %collective-permute-start.11 = (bf16[8,48,768]{2,1,0:T(8,128)(2,1)}, bf16[8,48,768]{2,1,0:T(8,128)(2,1)}, u32[]{:S(2)}, u32[]{:S(2)}) collective-permute-start(bf16[8,48,768]{2,1,0:T(8,128)(2,1)} %get-tuple-element.174), channel_id=1, source_target_pairs={{0,2},{2,0},{4,6},{6,4},{8,10},{10,8},{12,14},{14,12},{16,18},{18,... | collective-permute-start | bytes 1769480 | tf_op jit(solution)/shard_map/attend_back/ppermute | solution.py:755
  157.4 12.5 %collective-permute-start.17 = (bf16[2,48,1536]{2,1,0:T(8,128)(2,1)}, bf16[2,48,1536]{2,1,0:T(8,128)(2,1)S(1)}, u32[]{:S(2)}, u32[]{:S(2)}) collective-permute-start(bf16[2,48,1536]{2,1,0:T(8,128)(2,1)} %get-tuple-element.250), channel_id=1, source_target_pairs={{0,1},{1,0},{2,3},{3,2},{4,5},{5,4},{6,7},{7,6},{8,9},{9,8},{10,11... | collective-permute-start | bytes 884744 | tf_op jit(solution)/shard_map/rounds/ppermute | solution.py:680
  159.6 11.8 %collective-permute-start.15 = (bf16[2,48,2304]{2,1,0:T(8,128)(2,1)}, bf16[2,48,2304]{2,1,0:T(8,128)(2,1)S(1)}, u32[]{:S(2)}, u32[]{:S(2)}) collective-permute-start(bf16[2,48,2304]{2,1,0:T(8,128)(2,1)} %get-tuple-element.231), channel_id=1, source_target_pairs={{0,4},{2,6},{4,0},{6,2},{8,12},{10,14},{12,8},{14,10},{16,20},{18,... | collective-permute-start | bytes 1327112 | tf_op jit(solution)/shard_map/rounds/ppermute | solution.py:772
  161.5 8.3 %collective-permute-start.16 = (bf16[2,48,1536]{2,1,0:T(8,128)(2,1)}, bf16[2,48,1536]{2,1,0:T(8,128)(2,1)S(1)}, u32[]{:S(2)}, u32[]{:S(2)}) collective-permute-start(bf16[2,48,1536]{2,1,0:T(8,128)(2,1)} %get-tuple-element.236), channel_id=1, source_target_pairs={{0,8},{2,10},{4,12},{6,14},{8,0},{10,2},{12,4},{14,6},{16,24},{18,... | collective-permute-start | bytes 884744 | tf_op jit(solution)/shard_map/rounds/ppermute | solution.py:772
  168.6 18.4 %collective-permute-start.21 = (bf16[2,256,768]{2,1,0:T(8,128)(2,1)}, bf16[2,256,768]{2,1,0:T(8,128)(2,1)}, u32[]{:S(2)}, u32[]{:S(2)}) collective-permute-start(bf16[2,256,768]{2,1,0:T(8,128)(2,1)} %get-tuple-element.194), channel_id=1, source_target_pairs={{0,1},{1,0},{2,3},{3,2},{4,5},{5,4},{6,7},{7,6},{8,9},{9,8},{10,11... | collective-permute-start | bytes 2359304 | tf_op jit(solution)/shard_map/rounds/ppermute | solution.py:680
  171.7 6.3 %collective-permute-start.19 = (f32[16,128]{1,0:T(8,128)S(1)}, f32[16,128]{1,0:T(8,128)S(1)}, u32[]{:S(2)}, u32[]{:S(2)}) collective-permute-start(f32[16,128]{1,0:T(8,128)S(1)} %fusion.32), channel_id=1, source_target_pairs={{0,2},{2,0},{4,6},{6,4},{8,10},{10,8},{12,14},{14,12},{16,18},{18,... | collective-permute-start | bytes 24584 | tf_op jit(solution)/shard_map/small/ppermute | solution.py:980
  172.9 9.6 %collective-permute-start.18 = (bf16[4,48,768]{2,1,0:T(8,128)(2,1)S(1)}, bf16[4,48,768]{2,1,0:T(8,128)(2,1)S(1)}, u32[]{:S(2)}, u32[]{:S(2)}) collective-permute-start(bf16[4,48,768]{2,1,0:T(8,128)(2,1)S(1)} %bitcast.160), channel_id=1, source_target_pairs={{0,4},{2,6},{4,0},{6,2},{8,12},{10,14},{12,8},{14,10},{16,20},{18,... | collective-permute-start | bytes 884744 | tf_op jit(solution)/shard_map/rounds/ppermute | solution.py:772
  174.7 26.0 %collective-permute-start.23 = (bf16[1,48,3072]{2,1,0:T(8,128)(2,1)S(1)}, bf16[1,48,3072]{2,1,0:T(8,128)(2,1)S(1)}, u32[]{:S(2)}, u32[]{:S(2)}) collective-permute-start(bf16[1,48,3072]{2,1,0:T(8,128)(2,1)S(1)} %pad_maximum_fusion.5), channel_id=1, source_target_pairs={{0,16},{2,18},{4,20},{6,22},{8,24},{10,26},{12,28},{14,30},{16,0},... | collective-permute-start | bytes 884744 | tf_op jit(solution)/shard_map/rounds/ppermute | solution.py:772
  178.1 4.4 %collective-permute-start.20 = (f32[16,128]{1,0:T(8,128)S(1)}, f32[16,128]{1,0:T(8,128)S(1)}, u32[]{:S(2)}, u32[]{:S(2)}) collective-permute-start(f32[16,128]{1,0:T(8,128)S(1)} %fusion.42), channel_id=1, source_target_pairs={{0,4},{2,6},{4,0},{6,2},{8,12},{10,14},{12,8},{14,10},{16,20},{18,... | collective-permute-start | bytes 24584 | tf_op jit(solution)/shard_map/rounds/ppermute | solution.py:988
  180.7 20.0 %collective-permute-start.24 = (bf16[1,48,2304]{2,1,0:T(8,128)(2,1)}, bf16[1,48,2304]{2,1,0:T(8,128)(2,1)S(1)}, u32[]{:S(2)}, u32[]{:S(2)}) collective-permute-start(bf16[1,48,2304]{2,1,0:T(8,128)(2,1)} %fusion.12), channel_id=1, source_target_pairs={{0,16},{2,18},{4,20},{6,22},{8,24},{10,26},{12,28},{14,30},{16,0},... | collective-permute-start | bytes 663560 | tf_op jit(solution)/shard_map/rounds/ppermute | solution.py:772
  187.1 15.1 %collective-permute-start.22 = (bf16[2,48,768]{2,1,0:T(8,128)(2,1)S(1)}, bf16[2,48,768]{2,1,0:T(8,128)(2,1)S(1)}, u32[]{:S(2)}, u32[]{:S(2)}) collective-permute-start(bf16[2,48,768]{2,1,0:T(8,128)(2,1)S(1)} %get-tuple-element.248), channel_id=1, source_target_pairs={{0,8},{2,10},{4,12},{6,14},{8,0},{10,2},{12,4},{14,6},{16,24},{18,... | collective-permute-start | bytes 442376 | tf_op jit(solution)/shard_map/rounds/ppermute | solution.py:772
  188.3 13.9 %collective-permute-start.25 = (f32[16,128]{1,0:T(8,128)S(1)}, f32[16,128]{1,0:T(8,128)S(1)}, u32[]{:S(2)}, u32[]{:S(2)}) collective-permute-start(f32[16,128]{1,0:T(8,128)S(1)} %add.311), channel_id=1, source_target_pairs={{0,8},{2,10},{4,12},{6,14},{8,0},{10,2},{12,4},{14,6},{16,24},{18,... | collective-permute-start | bytes 24584 | tf_op jit(solution)/shard_map/rounds/ppermute | solution.py:988
  202.2 7.5 %collective-permute-start.29 = (f32[16,128]{1,0:T(8,128)S(1)}, f32[16,128]{1,0:T(8,128)S(1)}, u32[]{:S(2)}, u32[]{:S(2)}) collective-permute-start(f32[16,128]{1,0:T(8,128)S(1)} %add.319), channel_id=1, source_target_pairs={{0,16},{2,18},{4,20},{6,22},{8,24},{10,26},{12,28},{14,30},{16,0},... | collective-permute-start | bytes 24584 | tf_op jit(solution)/shard_map/rounds/ppermute | solution.py:988
  202.9 11.7 %collective-permute-start.28 = (bf16[48,3072]{1,0:T(8,128)(2,1)S(1)}, bf16[48,3072]{1,0:T(8,128)(2,1)S(1)}, u32[]{:S(2)}, u32[]{:S(2)}) collective-permute-start(bf16[48,3072]{1,0:T(8,128)(2,1)S(1)} %get-tuple-element.227), channel_id=1, source_target_pairs={{0,1},{1,0},{2,3},{3,2},{4,5},{5,4},{6,7},{7,6},{8,9},{9,8},{10,11... | collective-permute-start | bytes 884744 | tf_op jit(solution)/shard_map/rounds/ppermute | solution.py:680
  205.1 9.5 %collective-permute-start.27 = (bf16[48,2304]{1,0:T(8,128)(2,1)S(1)}, bf16[48,2304]{1,0:T(8,128)(2,1)S(1)}, u32[]{:S(2)}, u32[]{:S(2)}) collective-permute-start(bf16[48,2304]{1,0:T(8,128)(2,1)S(1)} %fusion.20), channel_id=1, source_target_pairs={{0,1},{1,0},{2,3},{3,2},{4,5},{5,4},{6,7},{7,6},{8,9},{9,8},{10,11... | collective-permute-start | bytes 663560 | tf_op jit(solution)/shard_map/rounds/ppermute | solution.py:680
  206.1 5.3 %collective-permute-start.26 = (bf16[1,48,768]{2,1,0:T(8,128)(2,1)S(1)}, bf16[1,48,768]{2,1,0:T(8,128)(2,1)S(1)}, u32[]{:S(2)}, u32[]{:S(2)}) collective-permute-start(bf16[1,48,768]{2,1,0:T(8,128)(2,1)S(1)} %fusion.22), channel_id=1, source_target_pairs={{0,16},{2,18},{4,20},{6,22},{8,24},{10,26},{12,28},{14,30},{16,0},... | collective-permute-start | bytes 221192 | tf_op jit(solution)/shard_map/rounds/ppermute | solution.py:772
  214.8 4.7 %collective-permute-start.31 = (f32[16,128]{1,0:T(8,128)S(1)}, f32[16,128]{1,0:T(8,128)S(1)}, u32[]{:S(2)}, u32[]{:S(2)}) collective-permute-start(f32[16,128]{1,0:T(8,128)S(1)} %add.321), channel_id=1, source_target_pairs={{0,1},{1,0},{2,3},{3,2},{4,5},{5,4},{6,7},{7,6},{8,9},{9,8},{10,11... | collective-permute-start | bytes 24584 | tf_op jit(solution)/shard_map/rounds/ppermute | solution.py:680
  216.4 4.4 %collective-permute-start.30 = (bf16[48,768]{1,0:T(8,128)(2,1)S(1)}, bf16[48,768]{1,0:T(8,128)(2,1)S(1)}, u32[]{:S(2)}, u32[]{:S(2)}) collective-permute-start(bf16[48,768]{1,0:T(8,128)(2,1)S(1)} %fusion.28), channel_id=1, source_target_pairs={{0,1},{1,0},{2,3},{3,2},{4,5},{5,4},{6,7},{7,6},{8,9},{9,8},{10,11... | collective-permute-start | bytes 221192 | tf_op jit(solution)/shard_map/rounds/ppermute | solution.py:680
  (32 other events, 138.8 us)
